TPU v7x, 128 devices: a whole 4x4x4 slice. The times are simulated.
128 devices in a mesh: tm: 8 (over x_lo, y), space: 16 (over z, x_hi, core).
Axes of the slice: x: 4 (x_hi: 2, x_lo: 2; x = x_hi * 2 + x_lo), y: 4, z: 4, core: 2. Of those that a mesh axis runs over, the one named last changes fastest.
Arguments:
- spatial_queries: bfloat16 [1, 16, 1024, 1536], P(None, 'tm', 'space'), may hold values from -40 to 40
- spatial_keys: bfloat16 [1, 16, 1024, 1536], P(None, 'tm', 'space'), may hold values from -40 to 40
- spatial_values: bfloat16 [1, 16, 1024, 1536], P(None, 'tm', 'space'), may hold values from -6 to 6
- temporal_queries: bfloat16 [1, 16, 1024, 1536], P(None, 'tm', 'space'), may hold values from -40 to 40
- temporal_keys: bfloat16 [1, 16, 1024, 1536], P(None, 'tm', 'space'), may hold values from -40 to 40
- temporal_values: bfloat16 [1, 16, 1024, 1536], P(None, 'tm', 'space'), may hold values from -6 to 6
- output_gradient: bfloat16 [1, 16, 1024, 3072], P(None, 'tm', 'space'), may hold values from -6 to 6
- spatial_projection: bfloat16 [1536, 3072], replicated, may hold values from -0.15625 to 0.15625
- temporal_projection: bfloat16 [1536, 3072], replicated, may hold values from -0.15625 to 0.15625
- adapter_down: bfloat16 [1536, 64], replicated, may hold values from -0.15625 to 0.15625
- adapter_up: bfloat16 [64, 3072], replicated, may hold values from -0.75 to 0.75
- spatial_channel_gate: float32 [3072], replicated, may hold values from 0.25 to 1.5
- temporal_channel_gate: float32 [3072], replicated, may hold values from 0.25 to 1.5
Outputs:
- grad_q_spatial: bfloat16 [1, 16, 1024, 1536], P(None, 'tm', 'space')
- grad_k_spatial: bfloat16 [1, 16, 1024, 1536], P(None, 'tm', 'space')
- grad_v_spatial: bfloat16 [1, 16, 1024, 1536], P(None, 'tm', 'space')
- grad_q_temporal: bfloat16 [1, 16, 1024, 1536], P(None, 'tm', 'space')
- grad_k_temporal: bfloat16 [1, 16, 1024, 1536], P(None, 'tm', 'space')
- grad_v_temporal: bfloat16 [1, 16, 1024, 1536], P(None, 'tm', 'space')
- grad_lora_down: float32 [1536, 64], replicated
- grad_lora_up: float32 [64, 3072], replicated
- grad_gate_spatial: float32 [3072], replicated
- grad_gate_temporal: float32 [3072], replicated
All inputs are finite; a program needn't handle non-finite values.
Results may differ from a plain program's by a relative error of at most 0.034.
Values may be sent and summed in bfloat16 or wider, within the bound.
A program may use at most 192 MiB of HBM per device.

v0:
```python
import jax
import jax.numpy as jnp
from jax import lax
from jax.sharding import PartitionSpec as P

LOCAL_HEADS = 12


def split_heads(tensor, temporal_pass):
    batch_count, frames, patches, feat_width = tensor.shape
    head_width = feat_width // LOCAL_HEADS
    tensor = tensor.reshape(batch_count, frames, patches, LOCAL_HEADS, head_width)
    if temporal_pass:
        return tensor.transpose(0, 2, 3, 1, 4).reshape(
            batch_count * patches * LOCAL_HEADS, frames, head_width
        )
    return tensor.transpose(0, 1, 3, 2, 4).reshape(
        batch_count * frames * LOCAL_HEADS, patches, head_width
    )


def join_heads(tensor, temporal_pass, batch_count, frames, patches):
    head_width = tensor.shape[-1]
    if temporal_pass:
        tensor = tensor.reshape(batch_count, patches, LOCAL_HEADS, frames, head_width).transpose(
            0, 3, 1, 2, 4
        )
    else:
        tensor = tensor.reshape(batch_count, frames, LOCAL_HEADS, patches, head_width).transpose(
            0, 1, 3, 2, 4
        )
    return tensor.reshape(batch_count, frames, patches, LOCAL_HEADS * head_width)


def attend(queries, key_items, value_items):
    head_scale = queries.shape[-1] ** (-0.5)
    scores = (
        jnp.einsum("nqe,nke->nqk", queries, key_items, preferred_element_type=jnp.float32)
        * head_scale
    )
    row_max = jnp.max(scores, axis=-1, keepdims=True)
    exp_scores = jnp.exp(scores - row_max)
    row_sum = jnp.sum(exp_scores, axis=-1, keepdims=True)
    prob_low = (exp_scores / row_sum).astype(jnp.bfloat16)
    attended = jnp.einsum("nqk,nke->nqe", prob_low, value_items, preferred_element_type=jnp.float32)
    return (attended.astype(jnp.bfloat16), row_max + jnp.log(row_sum))


def score_grads(queries, key_items, value_items, log_norm, grad_attended, row_dot, head_scale):
    scores = (
        jnp.einsum("nqe,nke->nqk", queries, key_items, preferred_element_type=jnp.float32)
        * head_scale
    )
    prob_back = jnp.exp(scores - log_norm)
    grad_probs = jnp.einsum(
        "nqe,nke->nqk", grad_attended, value_items, preferred_element_type=jnp.float32
    )
    grad_scores = (prob_back * (grad_probs - row_dot)).astype(jnp.bfloat16)
    return (grad_scores, prob_back.astype(jnp.bfloat16))


def attend_back(queries, key_items, value_items, attended, log_norm, grad_attended):
    head_scale = queries.shape[-1] ** (-0.5)
    row_dot = jnp.sum(
        grad_attended.astype(jnp.float32) * attended.astype(jnp.float32), axis=-1, keepdims=True
    )
    grad_scores, prob_low = score_grads(
        queries, key_items, value_items, log_norm, grad_attended, row_dot, head_scale
    )
    grad_query = (
        jnp.einsum("nqk,nke->nqe", grad_scores, key_items, preferred_element_type=jnp.float32)
        * head_scale
    )
    grad_key = (
        jnp.einsum("nqk,nqe->nke", grad_scores, queries, preferred_element_type=jnp.float32)
        * head_scale
    )
    grad_value = jnp.einsum(
        "nqk,nqe->nke", prob_low, grad_attended, preferred_element_type=jnp.float32
    )
    return (grad_query.astype(jnp.bfloat16), grad_key, grad_value)


def adapter_branch(
    attention_tokens, gradient_rows, projection_weight, adapter_down, adapter_up, gate_vector
):
    attention_rows = attention_tokens.reshape(-1, attention_tokens.shape[-1])
    contract_trailing = (((1,), (1,)), ((), ()))
    contract_first = (((0,), (0,)), ((), ()))
    lowrank_state = jnp.dot(
        attention_rows, adapter_down, preferred_element_type=jnp.float32
    ).astype(jnp.bfloat16)
    branch_output = jnp.dot(
        attention_rows, projection_weight, preferred_element_type=jnp.float32
    ) + jnp.dot(lowrank_state, adapter_up, preferred_element_type=jnp.float32)
    grad_wide = gradient_rows.astype(jnp.float32)
    gate_gradient = jnp.sum(grad_wide * branch_output, axis=0)
    branch_gradient = (grad_wide * gate_vector).astype(jnp.bfloat16)
    lowrank_gradient = lax.dot_general(
        branch_gradient, adapter_up, contract_trailing, preferred_element_type=jnp.float32
    ).astype(jnp.bfloat16)
    up_gradient = lax.dot_general(
        lowrank_state, branch_gradient, contract_first, preferred_element_type=jnp.float32
    )
    down_gradient = lax.dot_general(
        attention_rows, lowrank_gradient, contract_first, preferred_element_type=jnp.float32
    )
    attention_gradient = lax.dot_general(
        branch_gradient, projection_weight, contract_trailing, preferred_element_type=jnp.float32
    )
    attention_gradient = attention_gradient + lax.dot_general(
        lowrank_gradient, adapter_down, contract_trailing, preferred_element_type=jnp.float32
    )
    return (
        attention_gradient.astype(jnp.bfloat16).reshape(attention_tokens.shape),
        down_gradient,
        up_gradient,
        gate_gradient,
    )


def spatial_block(
    input_queries,
    input_keys,
    input_values,
    gradient_rows,
    projection_weight,
    adapter_down,
    adapter_up,
    gate_vector,
):
    batch_count, frames, patches, feat_width = input_queries.shape
    key_whole, value_whole = (
        lax.all_gather(input_keys, "space", axis=2, tiled=True),
        lax.all_gather(input_values, "space", axis=2, tiled=True),
    )
    queries = split_heads(input_queries, False)
    key_items = split_heads(key_whole, False)
    value_items = split_heads(value_whole, False)
    attended, log_norm = attend(queries, key_items, value_items)
    attention_tokens = join_heads(attended, False, batch_count, frames, patches)
    attention_gradient, down_gradient, up_gradient, gate_gradient = adapter_branch(
        attention_tokens, gradient_rows, projection_weight, adapter_down, adapter_up, gate_vector
    )
    grad_items = split_heads(attention_gradient, False)
    grad_query, grad_key, grad_value = attend_back(
        queries, key_items, value_items, attended, log_norm, grad_items
    )
    whole_patches = key_whole.shape[2]
    key_low = join_heads(grad_key.astype(jnp.bfloat16), False, batch_count, frames, whole_patches)
    value_low = join_heads(
        grad_value.astype(jnp.bfloat16), False, batch_count, frames, whole_patches
    )
    grad_key, grad_value = (
        lax.psum_scatter(key_low, "space", scatter_dimension=2, tiled=True).astype(jnp.float32),
        lax.psum_scatter(value_low, "space", scatter_dimension=2, tiled=True).astype(jnp.float32),
    )
    grad_key = grad_key.astype(jnp.bfloat16)
    grad_value = grad_value.astype(jnp.bfloat16)
    grads = (join_heads(grad_query, False, batch_count, frames, patches), grad_key, grad_value)
    return (grads, (down_gradient, up_gradient, gate_gradient))


def temporal_block(
    input_queries,
    input_keys,
    input_values,
    gradient_rows,
    projection_weight,
    adapter_down,
    adapter_up,
    gate_vector,
):
    batch_count, frames, patches, feat_width = input_queries.shape
    key_whole, value_whole = (
        lax.all_gather(input_keys, "tm", axis=1, tiled=True),
        lax.all_gather(input_values, "tm", axis=1, tiled=True),
    )
    queries = split_heads(input_queries, True)
    key_items = split_heads(key_whole, True)
    value_items = split_heads(value_whole, True)
    attended, log_norm = attend(queries, key_items, value_items)
    attention_tokens = join_heads(attended, True, batch_count, frames, patches)
    attention_gradient, down_gradient, up_gradient, gate_gradient = adapter_branch(
        attention_tokens, gradient_rows, projection_weight, adapter_down, adapter_up, gate_vector
    )
    grad_query, grad_key, grad_value = attend_back(
        queries, key_items, value_items, attended, log_norm, split_heads(attention_gradient, True)
    )
    whole_frames = key_whole.shape[1]
    key_low = join_heads(grad_key.astype(jnp.bfloat16), True, batch_count, whole_frames, patches)
    value_low = join_heads(
        grad_value.astype(jnp.bfloat16), True, batch_count, whole_frames, patches
    )
    grad_key, grad_value = (
        lax.psum_scatter(key_low, "tm", scatter_dimension=1, tiled=True).astype(jnp.float32),
        lax.psum_scatter(value_low, "tm", scatter_dimension=1, tiled=True).astype(jnp.float32),
    )
    grads = (
        join_heads(grad_query, True, batch_count, frames, patches),
        grad_key.astype(jnp.bfloat16),
        grad_value.astype(jnp.bfloat16),
    )
    return (grads, (down_gradient, up_gradient, gate_gradient))


def shards(
    spatial_queries,
    spatial_keys,
    spatial_values,
    temporal_queries,
    temporal_keys,
    temporal_values,
    output_gradient,
    spatial_projection,
    temporal_projection,
    adapter_down,
    adapter_up,
    spatial_channel_gate,
    temporal_channel_gate,
):
    gradient_rows = output_gradient.reshape(-1, output_gradient.shape[-1])
    spatial_gradients, space_terms = spatial_block(
        spatial_queries,
        spatial_keys,
        spatial_values,
        gradient_rows,
        spatial_projection,
        adapter_down,
        adapter_up,
        spatial_channel_gate,
    )
    space_terms = lax.psum((space_terms[0], space_terms[1], space_terms[2]), ("tm", "space"))
    temporal_gradients, time_terms = temporal_block(
        temporal_queries,
        temporal_keys,
        temporal_values,
        gradient_rows,
        temporal_projection,
        adapter_down,
        adapter_up,
        temporal_channel_gate,
    )
    time_terms = lax.psum((time_terms[0], time_terms[1], time_terms[2]), ("tm", "space"))
    down_total = space_terms[0] + time_terms[0]
    up_total = space_terms[1] + time_terms[1]
    gate_space_total = space_terms[2]
    gate_time_total = time_terms[2]
    return (
        spatial_gradients[0],
        spatial_gradients[1],
        spatial_gradients[2],
        temporal_gradients[0],
        temporal_gradients[1],
        temporal_gradients[2],
        down_total,
        up_total,
        gate_space_total,
        gate_time_total,
    )


def solution(mesh):
    placed = (
        P(None, "tm", "space", None),
        P(None, "tm", "space", None),
        P(None, "tm", "space", None),
        P(None, "tm", "space", None),
        P(None, "tm", "space", None),
        P(None, "tm", "space", None),
        P(None, "tm", "space", None),
        P(),
        P(),
        P(),
        P(),
        P(),
        P(),
    )
    return jax.shard_map(
        shards,
        mesh=mesh,
        in_specs=placed,
        out_specs=(
            P(None, "tm", "space", None),
            P(None, "tm", "space", None),
            P(None, "tm", "space", None),
            P(None, "tm", "space", None),
            P(None, "tm", "space", None),
            P(None, "tm", "space", None),
            P(),
            P(),
            P(),
            P(),
        ),
        check_vma=False,
    )
```

profile of v0, /device:TPU:0, one launch (start us, length us, event | category | flops | bytes accessed | tf_op | source)
XLA Modules:
  0.0 777.4 jit_solution(9838538006781359140)
XLA Ops:
  16.1 6.9 fusion.26
  23.7 54.1 %all-gather.5.cloned.1.call-done = bf16[1,2,1024,1536]{3,1,0,2:T(2,128)(2,1)} async-done(((bf16[1,2,64,1536]{3,1,0,2:T(2,128)(2,1)}), bf16[1,2,1024,1536]{3,1,0,2:T(2,128)(2,1)}) %all-gather.5.cloned.1.call-update) | async-done | bytes 6291472 | tf_op jit(solution)/shard_map/all_gather | solution.py:134
  77.8 16.7 %copy.75 = bf16[1,2,1024,1536]{2,3,1,0:T(8,128)(2,1)} copy(bf16[1,2,1024,1536]{3,1,0,2:T(2,128)(2,1)} %all-gather.5.cloned.1.call-done) | data formatting | bytes 12582912 | tf_op jit(solution)/shard_map/all_gather | solution.py:134
  94.6 48.3 %all-gather.7.cloned.1.call-done = bf16[1,2,1024,1536]{3,1,0,2:T(2,128)(2,1)} async-done(((bf16[1,2,64,1536]{3,1,0,2:T(2,128)(2,1)}), bf16[1,2,1024,1536]{3,1,0,2:T(2,128)(2,1)}) %all-gather.7.cloned.1.call-update) | async-done | bytes 6291472 | tf_op jit(solution)/shard_map/all_gather | solution.py:135
  142.9 16.2 %copy.79 = bf16[1,2,1024,1536]{2,3,1,0:T(8,128)(2,1)} copy(bf16[1,2,1024,1536]{3,1,0,2:T(2,128)(2,1)} %all-gather.7.cloned.1.call-done) | data formatting | bytes 12582912 | tf_op jit(solution)/shard_map/all_gather | solution.py:135
  159.1 4.2 multiply_reduce_fusion
  164.7 3.5 multiply_reduce_fusion.2
  172.3 4.4 multiply_convert_fusion
  176.8 16.4 %copy.82 = bf16[1,2,1024,1536]{3,1,0,2:T(2,128)(2,1)} copy(bf16[1,2,1024,1536]{2,3,1,0:T(8,128)(2,1)} %bitcast.145) | data formatting | bytes 12582912 | tf_op jit(solution)/shard_map/reshape | solution.py:32
  193.2 7.2 convolution_convert_fusion
  200.4 16.4 %copy.83 = bf16[1,2,1024,1536]{3,1,0,2:T(2,128)(2,1)} copy(bf16[1,2,1024,1536]{2,3,1,0:T(8,128)(2,1)} %bitcast.146) | data formatting | bytes 12582912 | tf_op jit(solution)/shard_map/reshape | solution.py:32
  217.9 7.0 fusion.21
  226.7 6.9 reshape.149
  233.6 7.5 copy.89
  241.1 6.9 reshape.146
  248.0 6.0 copy.86
  255.8 2.5 fusion.28
  258.5 11.1 %multiply_reduce_fusion.1 = (f32[768,2]{1,0:T(8,128)S(1)}, bf16[768,2,128]{2,1,0:T(2,128)(2,1)S(1)}) fusion(bf16[768,2,128]{2,1,0:T(2,128)(2,1)S(1)} %bitcast.179, bf16[768,16,128]{2,1,0:T(8,128)(2,1)S(1)} %bitcast.164, f32[768,2,16]{2,1,0:T(2,128)S(1)} %get-tuple-element.51, f32[768,2]{1,0:T(8,128)S(1)} %fusion.28, f32[768,2]{1,0:T(8,128)S(1)} %get-tuple-element.50), kind=kOutput, calls=%fused_computation.46 | convolution fusion | flops 7346688 | bytes 4048896 | tf_op jit(solution)/shard_map/nqk,nke->nqe/dot_general | solution.py:45
  269.6 2.8 fusion.16
  274.1 3.0 copy.128
  277.1 7.0 reshape.154
  284.1 4.0 convolution_convert_fusion.1
  288.2 3.0 copy.127
  291.2 6.9 reshape.156
  299.7 2.9 fusion.17
  304.1 5.2 fusion.31
  312.9 5.1 fusion.35
  318.1 6.1 fusion.15
  326.0 192.3 %all-reduce.2 = (f32[3072]{0:T(1024)}, f32[3072]{0:T(1024)}) all-reduce(f32[3072]{0:T(1024)S(1)} %fusion.12, f32[3072]{0:T(1024)S(1)} %fusion.13), channel_id=1, replica_groups=mesh['tm'=8,'space'=16] {'tm','space'}, use_global_device_ids=true, to_apply=%region_15.0 | all-reduce | flops 6144 | bytes 49152 | tf_op jit(solution)/shard_map/psum | solution.py:233
  521.5 42.3 %reduce-scatter.3.cloned.1.call-done = bf16[1,2,64,1536]{3,2,1,0:T(8,128)(2,1)} async-done(((bf16[1,16,64,1536]{3,2,1,0:T(8,128)(2,1)}), bf16[1,2,64,1536]{3,2,1,0:T(8,128)(2,1)}) %reduce-scatter.3.cloned.1.call-update) | async-done | bytes 393232 | tf_op jit(solution)/shard_map/reduce_scatter | solution.py:196
  563.8 48.9 %reduce-scatter.5.cloned.1.call-done = bf16[1,2,64,1536]{3,2,1,0:T(8,128)(2,1)} async-done(((bf16[1,16,64,1536]{3,2,1,0:T(8,128)(2,1)}), bf16[1,2,64,1536]{3,2,1,0:T(8,128)(2,1)}) %reduce-scatter.5.cloned.1.call-update) | async-done | bytes 393232 | tf_op jit(solution)/shard_map/reduce_scatter | solution.py:197
  612.7 153.6 %all-reduce.8.cloned.1.call-done = (f32[1536,64]{0,1:T(8,128)}, f32[64,3072]{1,0:T(8,128)}) async-done(((f32[1536,64]{0,1:T(8,128)}, f32[64,3072]{1,0:T(8,128)}), (f32[1536,64]{0,1:T(8,128)}, f32[64,3072]{1,0:T(8,128)})) %all-reduce.8.cloned.1.call-update) | async-done | bytes 1179664 | tf_op jit(solution)/shard_map/psum | solution.py:233
  (96 shorter events, 36.0 us)
Async XLA Ops:
  7.2 7.3 copy-start
  7.2 8.9 %copy-start.2 = (bf16[1,2,64,3072]{3,2,1,0:T(8,128)(2,1)S(1)}, bf16[1,2,64,3072]{3,2,1,0:T(8,128)(2,1)}, u32[]{:S(2)}) copy-start(bf16[1,2,64,3072]{3,2,1,0:T(8,128)(2,1)} %param.19) | copy-start | bytes 2359300
  7.2 8.9 %copy-start.11 = (f32[3072]{0:T(1024)S(1)}, f32[3072]{0:T(1024)}, u32[]{:S(2)}) copy-start(f32[3072]{0:T(1024)} %param.24) | copy-start | bytes 36868
  7.2 70.6 %all-gather.5.cloned.1.call-start = ((), (), s32[]{:S(2)}) async-start(), calls=%async_computation.2 | async-start | bytes 6684672 | tf_op jit(solution)/shard_map/all_gather | solution.py:134
  9.5 133.3 %all-gather.7.cloned.1.call-start = ((), (), s32[]{:S(2)}) async-start(), calls=%async_computation.3 | async-start | bytes 6684672 | tf_op jit(solution)/shard_map/all_gather | solution.py:135
  11.7 215.0 %all-gather.11.cloned.1.call-start = ((), (), s32[]{:S(2)}) async-start(), calls=%async_computation.5 | async-start | bytes 3538944 | tf_op jit(solution)/shard_map/all_gather | solution.py:177
  12.5 228.6 %all-gather.9.cloned.1.call-start = ((), (), s32[]{:S(2)}) async-start(), calls=%async_computation.4 | async-start | bytes 3538944 | tf_op jit(solution)/shard_map/all_gather | solution.py:176
  13.1 505.2 %all-reduce.10.cloned.1.call-start = ((), (), s32[]{:S(2)}) async-start(), calls=%async_computation.9 | async-start | bytes 25165824
  14.5 8.5 %copy-start.6 = (bf16[1536,64]{0,1:T(8,128)(2,1)S(1)}, bf16[1536,64]{0,1:T(8,128)(2,1)}, u32[]{:S(2)}) copy-start(bf16[1536,64]{0,1:T(8,128)(2,1)} %param.22) | copy-start | bytes 589828
  159.1 5.6 slice-start
  159.1 5.6 slice-start.1
  163.3 4.9 copy-start.1
  170.6 1.7 copy-start.3
  216.8 0.7 copy-start.12
  216.9 347.0 %reduce-scatter.3.cloned.1.call-start = ((), (), s32[]{:S(2)}) async-start(), calls=%async_computation.6 | async-start | bytes 3538944 | tf_op jit(solution)/shard_map/reduce_scatter | solution.py:196
  217.9 8.0 %copy-start.7 = (bf16[1,2,64,1536]{3,2,1,0:T(8,128)(2,1)S(1)}, bf16[1,2,64,1536]{3,2,1,0:T(8,128)(2,1)}, u32[]{:S(2)}) copy-start(bf16[1,2,64,1536]{3,2,1,0:T(8,128)(2,1)} %param.16) | copy-start | bytes 1179652
  248.0 10.5 %copy-start.5 = (bf16[1,64,12,16,128]{4,3,2,1,0:T(8,128)(2,1)S(1)}, bf16[1,64,12,16,128]{4,3,2,1,0:T(8,128)(2,1)}, u32[]{:S(2)}) copy-start(bf16[1,64,12,16,128]{4,3,2,1,0:T(8,128)(2,1)} %copy.89) | copy-start | bytes 9437188
  254.0 15.6 %copy-start.4 = (bf16[1,64,12,16,128]{4,3,2,1,0:T(8,128)(2,1)}, bf16[1,64,12,16,128]{4,3,2,1,0:T(8,128)(2,1)S(1)}, u32[]{:S(2)}) copy-start(bf16[1,64,12,16,128]{4,3,2,1,0:T(8,128)(2,1)S(1)} %copy.86) | copy-start | bytes 9437188
  258.4 11.2 %copy-start.9 = (f32[768,2]{1,0:T(8,128)}, f32[768,2]{1,0:T(8,128)S(1)}, u32[]{:S(2)}) copy-start(f32[768,2]{1,0:T(8,128)S(1)} %log_add_fusion) | copy-start | bytes 18436
  272.4 1.6 copy-start.14
  277.1 7.0 copy-start.10
  284.1 328.6 %reduce-scatter.5.cloned.1.call-start = ((), (), s32[]{:S(2)}) async-start(), calls=%async_computation.7 | async-start | bytes 3538944 | tf_op jit(solution)/shard_map/reduce_scatter | solution.py:197
  291.2 7.3 copy-start.13
  291.2 8.5 %copy-start.15 = (bf16[768,2,16]{2,1,0:T(2,128)(2,1)S(1)}, bf16[768,2,16]{2,1,0:T(2,128)(2,1)}, u32[]{:S(2)}) copy-start(bf16[768,2,16]{2,1,0:T(2,128)(2,1)} %copy-done.14) | copy-start | bytes 147460
  298.2 468.1 %all-reduce.8.cloned.1.call-start = ((), (), s32[]{:S(2)}) async-start(), calls=%async_computation.8 | async-start | bytes 2359296 | tf_op jit(solution)/shard_map/psum | solution.py:233
  304.1 5.7 copy-start.8
Sparse Core Ops, SparseCore 0:
  11.1 66.7 all-gather.4
  80.9 61.9 all-gather.6
  144.5 41.8 all-gather.10
  187.9 43.8 all-gather.8
  234.3 283.6 all-reduce.9
  520.8 42.9 reduce-scatter.2
  566.8 45.8 reduce-scatter.4
  618.1 148.0 all-reduce.7
where the time goes:
time: 784 us; the launch traced here: 777 us
  waiting for transfers between devices  349 us (45%)
  blocking collectives  192 us (24%)
  local copies, waits for them, and re-layouts  133 us (17%)
  matrix products  83 us (11%)
  between operations  15.7 us (2%)
    psum x1, blocking collectives, shards(): lax.psum((space_terms[0], space_terms[1], space_terms[2]), ('tm', 'space'))  192 us
    psum x1, waiting for transfers between devices, shards(): lax.psum((space_terms[0], space_terms[1], space_terms[2]), ('tm', 'space'))  154 us
    all_gather x1, waiting for transfers between devices, spatial_block(): lax.all_gather(input_keys, 'space', axis=2, tiled=True)  54.1 us
    reduce_scatter x1, waiting for transfers between devices, temporal_block(): lax.psum_scatter(value_low, 'tm', scatter_dimension=1, tiled=True)  48.9 us
    reshape x6, local copies, waits for them, and re-layouts, join_heads(): tensor.reshape(batch_count, frames, patches, LOCAL_HEADS * head_width)  48.8 us
    all_gather x1, waiting for transfers between devices, spatial_block(): lax.all_gather(input_values, 'space', axis=2, tiled=True)  48.3 us
    reduce_scatter x1, waiting for transfers between devices, temporal_block(): lax.psum_scatter(key_low, 'tm', scatter_dimension=1, tiled=True)  42.3 us
    all_gather x1, local copies, waits for them, and re-layouts, spatial_block(): lax.all_gather(input_keys, 'space', axis=2, tiled=True)  16.7 us
  transfers between devices with their start and end apart: 8, of which 5 were waited for; matrix products, arithmetic and copies ran while one was open for 27% of the time, Pallas kernels for 0%

commit v1 on v0

v1 whole, which is shorter than its diff:
```python
import jax
import jax.numpy as jnp
from jax import lax
from jax.experimental import pallas as pl
from jax.experimental.pallas import tpu as pltpu
from jax.sharding import PartitionSpec as P

MESH = pl.DeviceIdType.MESH
BF = jnp.bfloat16
F32 = jnp.float32
SCALE = 128 ** (-0.5)
NN = (((1,), (0,)), ((), ()))
NT = (((1,), (1,)), ((), ()))
TN = (((0,), (0,)), ((), ()))
ROWS = 2688
PART = 336
PIECE = 24


def dot(a, b, dims):
    return lax.dot_general(a, b, dims, preferred_element_type=F32)


def aligned(value, unit):
    return pl.multiple_of(value, unit)


def kernel(
    sq, sk, sv, tq, tk, tv, og_hbm, ws_hbm, wt_hbm, down_hbm, up_hbm, gs_hbm, gt_hbm,
    o_sq, o_sk, o_sv, o_tq, o_tk, o_tv, o_down, o_up, o_gs, o_gt,
    sr, so, prob, dsc, tr, to, og, ws, wt, down, up, gs, gt, gb, glow, ga_s, ga_t, ah_s, ah_t,
    low, gate_rows, pr, r1, acc, r2, s2, r3, b4, r4,
    load_sem, s_in, s_out, t_in, t_out, s_home, s_back, t_home, t_back, red_in, red_out,
):
    t = lax.axis_index("tm")
    s = lax.axis_index("space")
    chip = s // 2
    core = lax.rem(s, 2)
    z = s // 4
    xh = lax.rem(chip, 2)
    ia = z * 2 + core
    ib = xh * 8 + t

    loads = [
        pltpu.make_async_copy(src, dst, load_sem.at[n])
        for n, (src, dst) in enumerate(
            ((og_hbm, og), (gs_hbm, gs), (gt_hbm, gt), (up_hbm, up), (down_hbm, down), (ws_hbm, ws), (wt_hbm, wt))
        )
    ]
    for load in loads:
        load.start()

    gate = pltpu.get_barrier_semaphore()

    def greet(device):
        pl.semaphore_signal(gate, inc=1, device_id=device, device_id_type=MESH)

    def greet_space(n, carry):
        greet((t, lax.rem(s + n, 16)))
        return carry

    def greet_tm(n, carry):
        other = lax.rem(t + n, 8)
        greet((other, s))
        greet((other, z * 4 + (1 - xh) * 2 + core))
        return carry

    lax.fori_loop(1, 16, greet_space, 0)
    lax.fori_loop(1, 8, greet_tm, 0)
    pl.semaphore_wait(gate, 29)

    def start_local(src, dst, sem):
        pltpu.make_async_copy(src, dst, sem).start()

    def start_remote(src, dst, send, recv, device):
        pltpu.make_async_remote_copy(
            src, dst, send, recv, device_id=device, device_id_type=MESH
        ).start()

    def await_bytes(ref, sem):
        pltpu.make_async_copy(ref, ref, sem).wait()

    WIDTH = (256, 128)

    def spatial_out(src, i):
        def ends(d, k):
            col = aligned(lax.rem(d, 4) * 384 + k * 256, 128)
            return (
                src.at[d // 4, :, pl.ds(col, WIDTH[k])],
                sr.at[i, pl.ds(aligned(s * 64, 64), 64), pl.ds(0, WIDTH[k])],
            )

        def step(n, carry):
            d = lax.rem(chip + n, 8)
            for k in (0, 1):
                a, b = ends(d, k)
                start_remote(a, b, s_out.at[i], s_in.at[i], (t, d * 2 + k))
            return carry

        lax.fori_loop(1, 8, step, 0)
        for k in (0, 1):
            a, b = ends(chip, k)

            @pl.when(core == k)
            def _():
                start_local(a, b, s_in.at[i])

            @pl.when(core != k)
            def _():
                start_remote(a, b, s_out.at[i], s_in.at[i], (t, chip * 2 + k))

    def spatial_arrived(i):
        @pl.when(core == 0)
        def _():
            await_bytes(sr.at[i], s_in.at[i])

        @pl.when(core == 1)
        def _():
            await_bytes(sr.at[i, :, pl.ds(0, 128)], s_in.at[i])

    def spatial_back(j, home):
        for k in (0, 1):

            @pl.when(core == k)
            def _():
                col = aligned(lax.rem(chip, 4) * 384 + k * 256, 128)
                dst = home.at[chip // 4, :, pl.ds(col, WIDTH[k])]

                def src(d):
                    return so.at[j, pl.ds(aligned(d * 64, 64), 64), pl.ds(0, WIDTH[k])]

                def step(n, carry):
                    d = lax.rem(s + n, 16)
                    start_remote(src(d), dst, s_back.at[j], s_home.at[j], (t, d))
                    return carry

                lax.fori_loop(1, 16, step, 0)
                start_local(src(s), dst, s_home.at[j])

    def temporal_out(src, i):
        def ends(d):
            row = aligned(lax.rem(d, 4) * 16, 16)
            col = aligned((d // 4) * 768, 128)
            return src.at[:, pl.ds(row, 16), pl.ds(col, 768)], tr.at[i, pl.ds(2 * t, 2)]

        def step(n, carry):
            d = lax.rem(t + n, 8)
            a, b = ends(d)
            start_remote(a, b, t_out.at[i], t_in.at[i], (d, s))
            return carry

        lax.fori_loop(1, 8, step, 0)
        a, b = ends(t)
        start_local(a, b, t_in.at[i])

    def temporal_back(j, home):
        row = aligned(lax.rem(t, 4) * 16, 16)
        col = aligned((t // 4) * 768, 128)
        dst = home.at[:, pl.ds(row, 16), pl.ds(col, 768)]

        def step(n, carry):
            d = lax.rem(t + n, 8)
            start_remote(to.at[j, pl.ds(2 * d, 2)], dst, t_back.at[j], t_home.at[j], (d, s))
            return carry

        lax.fori_loop(1, 8, step, 0)
        start_local(to.at[j, pl.ds(2 * t, 2)], dst, t_home.at[j])

    for i, src in enumerate((sq, sk, sv)):
        spatial_out(src, i)

    def attention_gradient(b, channel_gate, weight, weight_load, home):
        branch = (og[...].astype(F32) * channel_gate[...]).astype(BF)
        gb[b] = branch
        small = dot(branch, up[...], NT).astype(BF)
        glow[b] = small
        weight_load.wait()

        def step(n, carry):
            rows = pl.ds(aligned(n * 256, 256), 256)
            part = dot(gb[b], weight[rows, :], NT) + dot(small, down[rows, :], NT)
            home[:, :, rows] = part.astype(BF).reshape(2, 64, 256)
            return carry

        lax.fori_loop(0, 6, step, 0)

    for load in loads[:5]:
        load.wait()
    attention_gradient(0, gs, ws, loads[5], ga_s)
    spatial_out(ga_s, 3)
    for i, src in enumerate((tq, tk, tv)):
        temporal_out(src, i)
    attention_gradient(1, gt, wt, loads[6], ga_t)
    temporal_out(ga_t, 3)

    heads = 2 - core
    for i in range(3):
        spatial_arrived(i)

    def spatial_forward(h, carry):
        c = pl.ds(aligned(h * 128, 128), 128)
        keys = sr[1, :, c]
        values = sr[2, :, c]
        for n in range(4):
            r = pl.ds(n * 256, 256)
            scores = dot(sr[0, r, c], keys, NT) * SCALE
            expd = jnp.exp(scores - jnp.max(scores, axis=1, keepdims=True))
            total = jnp.sum(expd, axis=1, keepdims=True)
            low_prob = (expd * (1.0 / total)).astype(BF)
            prob[h, r, :] = low_prob
            so[0, r, c] = dot(low_prob, values, NN).astype(BF)
        return carry

    lax.fori_loop(0, heads, spatial_forward, 0)
    spatial_back(0, ah_s)

    spatial_arrived(3)

    def spatial_backward(h, carry):
        c = pl.ds(aligned(h * 128, 128), 128)
        keys = sr[1, :, c]
        values = sr[2, :, c]
        for n in range(4):
            r = pl.ds(n * 256, 256)
            grad = sr[3, r, c]
            row_dot = jnp.sum(
                grad.astype(F32) * so[0, r, c].astype(F32), axis=1, keepdims=True
            )
            grad_prob = dot(grad, values, NT)
            grad_scores = (prob[h, r, :].astype(F32) * (grad_prob - row_dot)).astype(BF)
            dsc[r, :] = grad_scores
            so[1, r, c] = (dot(grad_scores, keys, NN) * SCALE).astype(BF)
        queries_t = sr[0, :, c].T
        grads_t = sr[3, :, c].T
        for n in range(4):
            r = pl.ds(n * 256, 256)
            so[2, r, c] = (dot(queries_t, dsc[:, r], NN) * SCALE).T.astype(BF)
            so[3, r, c] = dot(grads_t, prob[h, :, r], NN).T.astype(BF)
        return carry

    lax.fori_loop(0, heads, spatial_backward, 0)
    for j, home in ((1, o_sq), (2, o_sk), (3, o_sv)):
        spatial_back(j, home)

    for i in range(4):
        await_bytes(tr.at[i], t_in.at[i])
    same_patch = lax.rem(lax.broadcasted_iota(jnp.int32, (256, 256), 0), 16) == lax.rem(
        lax.broadcasted_iota(jnp.int32, (256, 256), 1), 16
    )

    def temporal_head(h, carry):
        c = pl.ds(aligned(h * 128, 128), 128)
        queries, keys, values, grad = (tr[i, :, :, c].reshape(256, 128) for i in range(4))
        scores = jnp.where(same_patch, dot(queries, keys, NT) * SCALE, -1e30)
        expd = jnp.exp(scores - jnp.max(scores, axis=1, keepdims=True))
        total = jnp.sum(expd, axis=1, keepdims=True)
        probs = expd * (1.0 / total)
        low_prob = probs.astype(BF)
        attended = dot(low_prob, values, NN).astype(BF)
        row_dot = jnp.sum(grad.astype(F32) * attended.astype(F32), axis=1, keepdims=True)
        grad_scores = (probs * (dot(grad, values, NT) - row_dot)).astype(BF)
        out = (
            attended,
            (dot(grad_scores, keys, NN) * SCALE).astype(BF),
            (dot(grad_scores, queries, TN) * SCALE).astype(BF),
            dot(low_prob, grad, TN).astype(BF),
        )
        for j in range(4):
            to[j, :, :, c] = out[j].reshape(16, 16, 128)
        return carry

    lax.fori_loop(0, 6, temporal_head, 0)
    for j, home in ((0, ah_t), (1, o_tq), (2, o_tk), (3, o_tv)):
        temporal_back(j, home)

    def adapter(b, home, arrived, weight):
        await_bytes(home, arrived)
        rows = home[...].reshape(128, 1536)
        small = dot(rows, down[...], NN).astype(BF)
        low[b] = small

        def step(n, carry):
            c = pl.ds(aligned(n * 512, 512), 512)
            branch = dot(home[...].reshape(128, 1536), weight[:, c], NN) + dot(low[b], up[:, c], NN)
            gate_rows[b, :, c] = jnp.sum(og[:, c].astype(F32) * branch, axis=0, keepdims=True)
            return carry

        lax.fori_loop(0, 6, step, 0)

    adapter(0, ah_s, s_home.at[0], ws)
    adapter(1, ah_t, t_home.at[0], wt)

    low_st = low[0].astype(F32).T.astype(BF)
    low_tt = low[1].astype(F32).T.astype(BF)
    glow_st = glow[0].astype(F32).T.astype(BF)
    glow_tt = glow[1].astype(F32).T.astype(BF)
    line = lax.broadcasted_iota(jnp.int32, (16, 128), 0)
    for j in range(24):
        c = pl.ds(j * 128, 128)
        pr[pl.ds(j * 80, 64), :] = (
            dot(low_st, gb[0, :, c], NN) + dot(low_tt, gb[1, :, c], NN)
        ).astype(BF)
        pr[pl.ds(j * 80 + 64, 16), :] = jnp.where(
            line == 0, gate_rows[0, :, c], jnp.where(line == 1, gate_rows[1, :, c], 0.0)
        ).astype(BF)
    for j in range(12):
        c = pl.ds(j * 128, 128)
        pr[pl.ds(1920 + j * 64, 64), :] = (
            dot(glow_st, ah_s[:, :, c].reshape(128, 128), NN)
            + dot(glow_tt, ah_t[:, :, c].reshape(128, 128), NN)
        ).astype(BF)

    def in_a(j):
        return (t, (j // 2) * 4 + xh * 2 + lax.rem(j, 2))

    def in_b(j):
        return (lax.rem(j, 8), z * 4 + (j // 8) * 2 + core)

    def exchange(stage, size, mine, device, src, dst):
        def step(n, carry):
            j = lax.rem(mine + n, size)
            start_remote(src(j), dst, red_out.at[stage], red_in.at[stage], device(j))
            return carry

        lax.fori_loop(1, size, step, 0)
        start_local(src(mine), dst, red_in.at[stage])

    exchange(
        0, 8, ia, in_a,
        lambda j: pr.at[pl.ds(aligned(j * PART, 16), PART), :],
        r1.at[ia],
    )
    await_bytes(r1, red_in.at[0])
    total = r1[0].astype(F32)
    for n in range(1, 8):
        total = total + r1[n].astype(F32)
    acc[pl.ds(0, PART), :] = total
    acc[pl.ds(PART, 16 * PIECE - PART), :] = jnp.zeros((16 * PIECE - PART, 128), F32)

    exchange(
        1, 16, ib, in_b,
        lambda j: acc.at[pl.ds(aligned(j * PIECE, 8), PIECE), :],
        r2.at[ib],
    )
    await_bytes(r2, red_in.at[1])
    total = r2[0]
    for n in range(1, 16):
        total = total + r2[n]
    s2[...] = total

    exchange(2, 16, ib, in_b, lambda j: s2, r3.at[pl.ds(aligned(ib * PIECE, 8), PIECE), :])
    await_bytes(r3, red_in.at[2])
    b4[...] = r3[pl.ds(0, PART), :].astype(BF)

    exchange(3, 8, ia, in_a, lambda j: b4, r4.at[pl.ds(aligned(ia * PART, 16), PART), :])
    await_bytes(r4, red_in.at[3])
    for j in range(24):
        c = pl.ds(j * 128, 128)
        o_up[:, c] = r4[pl.ds(j * 80, 64), :].astype(F32)
        tail = r4[pl.ds(j * 80 + 64, 16), :].astype(F32)
        o_gs[:, c] = tail[0:1]
        o_gt[:, c] = tail[1:2]
    for j in range(12):
        o_down[pl.ds(j * 128, 128), :] = r4[pl.ds(1920 + j * 64, 64), :].astype(F32).T

    for j, (s_ref, t_ref) in enumerate(((None, None), (o_sq, o_tq), (o_sk, o_tk), (o_sv, o_tv))):
        if j > 0:
            await_bytes(s_ref, s_home.at[j])
            await_bytes(t_ref, t_home.at[j])
    for i in range(4):
        await_bytes(tr.at[0, pl.ds(0, 14)], t_out.at[i])
        await_bytes(to.at[0, pl.ds(0, 14)], t_back.at[i])
        for k in (0, 1):

            @pl.when(core == k)
            def _():
                await_bytes(og.at[pl.ds(0, 64), pl.ds(0, 3072 - WIDTH[k])], s_out.at[i])
                await_bytes(so.at[0, pl.ds(0, 960), pl.ds(0, WIDTH[k])], s_back.at[i])

    await_bytes(pr.at[pl.ds(0, 7 * PART), :], red_out.at[0])
    await_bytes(acc.at[pl.ds(0, 15 * PIECE), :], red_out.at[1])
    await_bytes(acc.at[pl.ds(0, 15 * PIECE), :], red_out.at[2])
    await_bytes(pr.at[pl.ds(0, 7 * PART), :], red_out.at[3])


def shards(
    spatial_queries,
    spatial_keys,
    spatial_values,
    temporal_queries,
    temporal_keys,
    temporal_values,
    output_gradient,
    spatial_projection,
    temporal_projection,
    adapter_down,
    adapter_up,
    spatial_channel_gate,
    temporal_channel_gate,
):
    tokens = jax.ShapeDtypeStruct((2, 64, 1536), BF)
    dma = pltpu.SemaphoreType.DMA
    outs = pl.pallas_call(
        kernel,
        out_shape=(tokens,) * 6
        + (
            jax.ShapeDtypeStruct((1536, 64), F32),
            jax.ShapeDtypeStruct((64, 3072), F32),
            jax.ShapeDtypeStruct((1, 3072), F32),
            jax.ShapeDtypeStruct((1, 3072), F32),
        ),
        in_specs=[pl.BlockSpec(memory_space=pl.ANY)] * 13,
        out_specs=[pl.BlockSpec(memory_space=pl.ANY)] * 6
        + [pl.BlockSpec(memory_space=pltpu.VMEM)] * 4,
        scratch_shapes=[
            pltpu.VMEM((4, 1024, 256), BF),
            pltpu.VMEM((4, 1024, 256), BF),
            pltpu.VMEM((2, 1024, 1024), BF),
            pltpu.VMEM((1024, 1024), BF),
            pltpu.VMEM((4, 16, 16, 768), BF),
            pltpu.VMEM((4, 16, 16, 768), BF),
            pltpu.VMEM((128, 3072), BF),
            pltpu.VMEM((1536, 3072), BF),
            pltpu.VMEM((1536, 3072), BF),
            pltpu.VMEM((1536, 64), BF),
            pltpu.VMEM((64, 3072), BF),
            pltpu.VMEM((1, 3072), F32),
            pltpu.VMEM((1, 3072), F32),
            pltpu.VMEM((2, 128, 3072), BF),
            pltpu.VMEM((2, 128, 64), BF),
            pltpu.VMEM((2, 64, 1536), BF),
            pltpu.VMEM((2, 64, 1536), BF),
            pltpu.VMEM((2, 64, 1536), BF),
            pltpu.VMEM((2, 64, 1536), BF),
            pltpu.VMEM((2, 128, 64), BF),
            pltpu.VMEM((2, 1, 3072), F32),
            pltpu.VMEM((ROWS, 128), BF),
            pltpu.VMEM((8, PART, 128), BF),
            pltpu.VMEM((16 * PIECE, 128), F32),
            pltpu.VMEM((16, PIECE, 128), F32),
            pltpu.VMEM((PIECE, 128), F32),
            pltpu.VMEM((16 * PIECE, 128), F32),
            pltpu.VMEM((PART, 128), BF),
            pltpu.VMEM((ROWS, 128), BF),
            dma((7,)),
            dma((4,)),
            dma((4,)),
            dma((4,)),
            dma((4,)),
            dma((4,)),
            dma((4,)),
            dma((4,)),
            dma((4,)),
            dma((4,)),
            dma((4,)),
        ],
        compiler_params=pltpu.CompilerParams(
            collective_id=0, has_side_effects=True, vmem_limit_bytes=56 << 20
        ),
    )(
        *(
            array.reshape(2, 64, 1536)
            for array in (
                spatial_queries,
                spatial_keys,
                spatial_values,
                temporal_queries,
                temporal_keys,
                temporal_values,
            )
        ),
        output_gradient.reshape(128, 3072),
        spatial_projection,
        temporal_projection,
        adapter_down,
        adapter_up,
        spatial_channel_gate.reshape(1, 3072),
        temporal_channel_gate.reshape(1, 3072),
    )
    return (
        *(array.reshape(1, 2, 64, 1536) for array in outs[:6]),
        outs[6],
        outs[7],
        outs[8].reshape(3072),
        outs[9].reshape(3072),
    )


def solution(mesh):
    tokens = P(None, "tm", "space", None)
    return jax.shard_map(
        shards,
        mesh=mesh,
        in_specs=(tokens,) * 7 + (P(),) * 6,
        out_specs=(tokens,) * 6 + (P(),) * 4,
        check_vma=False,
    )
```

time: 784 us -> 126 us (0.16)
  waiting for transfers between devices: 349 us -> 0 us
  blocking collectives: 192 us -> 0 us
  local copies, waits for them, and re-layouts: 133 us -> 19.3 us
  Pallas kernels: 0 us -> 103 us
  matrix products: 83 us -> 0 us
  between operations: 15.7 us -> 0.66 us
    psum x1 -> x0, blocking collectives: 192 us -> none  [shards(): lax.psum((space_terms[0], space_terms[1], space_terms[2]), ('tm', 'space'))]
    psum x1 -> x0, waiting for transfers between devices: 154 us -> none  [shards(): lax.psum((space_terms[0], space_terms[1], space_terms[2]), ('tm', 'space'))]
    pallas_call x0 -> x1, Pallas kernels: none -> 103 us  [shards(): pl.pallas_call(kernel, out_shape=(tokens,) * 6 + (jax.ShapeDtypeStruct((1...]
    all_gather x4 -> x0, waiting for transfers between devices: 102 us -> none  [the longest x1 54.1 us: spatial_block(): lax.all_gather(input_keys, 'space', axis=2, tiled=True)]
    reduce_scatter x2 -> x0, waiting for transfers between devices: 91.2 us -> none  [the longest x1 48.9 us: temporal_block(): lax.psum_scatter(value_low, 'tm', scatter_dimension=1, tiled=True)]
    dot_general x28 -> x0, matrix products: 83 us -> none  [the longest x2 14.6 us: attend(): jnp.einsum('nqk,nke->nqe', prob_low, value_items, preferred_element_type=...]
    reshape x16 -> x0, local copies, waits for them, and re-layouts: 70.9 us -> none  [the longest x6 48.8 us: join_heads(): tensor.reshape(batch_count, frames, patches, LOCAL_HEADS * head_width)]
    all_gather x2 -> x0, local copies, waits for them, and re-layouts: 32.9 us -> none  [the longest x1 16.7 us: spatial_block(): lax.all_gather(input_keys, 'space', axis=2, tiled=True)]
  transfers between devices with their start and end apart: 8 -> 0, of which waited for: 5 -> 0; matrix products, arithmetic and copies ran while one was open for 27% -> 0% of each run, Pallas kernels for 0% -> 0%
where the time goes in v1:
time: 126 us; the launch traced here: 123 us
  Pallas kernels  103 us (82%)
  local copies, waits for them, and re-layouts  19.3 us (15%)
    pallas_call x1, Pallas kernels, shards(): pl.pallas_call(kernel, out_shape=(tokens,) * 6 + (jax.ShapeDtypeStruct((1...  103 us
    unnamed x11, local copies, waits for them, and re-layouts  19.3 us

profile of v1, /device:TPU:0, one launch (start us, length us, event | category | flops | bytes accessed | tf_op | source)
XLA Modules:
  0.0 123.3 jit_solution(18222877337910489891)
XLA Ops:
  0.6 1.8 %copy.23.down_hbm = bf16[1536,64]{1,0:T(8,128)(2,1)} copy(bf16[1536,64]{0,1:T(8,128)(2,1)} %param.22) | data formatting | bytes 393216 | tf_op args[9]
  2.5 103.4 %shard_map.204 = (bf16[2,64,1536]{2,1,0:T(8,128)(2,1)}, bf16[2,64,1536]{2,1,0:T(8,128)(2,1)}, bf16[2,64,1536]{2,1,0:T(8,128)(2,1)}, bf16[2,64,1536]{2,1,0:T(8,12...) custom-call(bf16[2,64,1536]{2,1,0:T(8,128)(2,1)} %bitcast.24, ...), custom_call_target="tpu_custom_call" | custom-call | tf_op jit(solution)/shard_map/pallas_call | solution.py:403
  105.9 2.1 %copy.24 = f32[1536,64]{0,1:T(8,128)} copy(f32[1536,64]{1,0:T(8,128)} %get-tuple-element.36) | data formatting | bytes 786432
  108.1 1.8 %copy.34 = bf16[1,2,64,1536]{3,2,1,0:T(8,128)(2,1)} copy(bf16[1,2,64,1536]{3,2,1,0:T(8,128)(2,1)} %bitcast.23) | data formatting | bytes 786432
  109.8 1.8 %copy.35 = bf16[1,2,64,1536]{3,2,1,0:T(8,128)(2,1)} copy(bf16[1,2,64,1536]{3,2,1,0:T(8,128)(2,1)} %bitcast.22) | data formatting | bytes 786432
  111.6 1.8 %copy.36 = bf16[1,2,64,1536]{3,2,1,0:T(8,128)(2,1)} copy(bf16[1,2,64,1536]{3,2,1,0:T(8,128)(2,1)} %bitcast.21) | data formatting | bytes 786432
  113.4 1.8 %copy.37 = bf16[1,2,64,1536]{3,2,1,0:T(8,128)(2,1)} copy(bf16[1,2,64,1536]{3,2,1,0:T(8,128)(2,1)} %bitcast.20) | data formatting | bytes 786432
  115.1 1.8 %copy.38 = bf16[1,2,64,1536]{3,2,1,0:T(8,128)(2,1)} copy(bf16[1,2,64,1536]{3,2,1,0:T(8,128)(2,1)} %bitcast.19) | data formatting | bytes 786432
  116.9 1.8 %copy.39 = bf16[1,2,64,1536]{3,2,1,0:T(8,128)(2,1)} copy(bf16[1,2,64,1536]{3,2,1,0:T(8,128)(2,1)} %bitcast.18) | data formatting | bytes 786432
  118.7 2.1 %copy.40 = f32[64,3072]{1,0:T(8,128)} copy(f32[64,3072]{1,0:T(8,128)} %get-tuple-element.57) | data formatting | bytes 1572864
  120.7 1.3 %copy.41 = f32[3072]{0:T(1024)} copy(f32[3072]{0:T(1024)} %bitcast.33) | data formatting | bytes 24576
  122.0 1.3 %copy.42 = f32[3072]{0:T(1024)} copy(f32[3072]{0:T(1024)} %bitcast.32) | data formatting | bytes 24576

commit v2 on v1

--- a/solution.py
+++ b/solution.py
@@ -27,9 +27,9 @@
 
 def kernel(
     sq, sk, sv, tq, tk, tv, og_hbm, ws_hbm, wt_hbm, down_hbm, up_hbm, gs_hbm, gt_hbm,
-    o_sq, o_sk, o_sv, o_tq, o_tk, o_tv, o_down, o_up, o_gs, o_gt,
-    sr, so, prob, dsc, tr, to, og, ws, wt, down, up, gs, gt, gb, glow, ga_s, ga_t, ah_s, ah_t,
-    low, gate_rows, pr, r1, acc, r2, s2, r3, b4, r4,
+    o_sq, o_sk, o_sv, o_tq, o_tk, o_tv, r4,
+    sr, so, prob, dsc, tr, to, tprob, og, ws, wt, down, up, gs, gt, gb, glow, ga_s, ga_t, ah_s, ah_t,
+    low, gate_rows, pr, r1, acc, r2, s2, r3, b4,
     load_sem, s_in, s_out, t_in, t_out, s_home, s_back, t_home, t_back, red_in, red_out,
 ):
     t = lax.axis_index("tm")
@@ -178,18 +178,18 @@
 
         def step(n, carry):
             rows = pl.ds(aligned(n * 256, 256), 256)
-            part = dot(gb[b], weight[rows, :], NT) + dot(small, down[rows, :], NT)
+            part = dot(gb[b], weight[rows, :], NT) + dot(small, down[:, rows], NN)
             home[:, :, rows] = part.astype(BF).reshape(2, 64, 256)
             return carry
 
         lax.fori_loop(0, 6, step, 0)
 
+    for i, src in enumerate((tq, tk, tv)):
+        temporal_out(src, i)
     for load in loads[:5]:
         load.wait()
     attention_gradient(0, gs, ws, loads[5], ga_s)
     spatial_out(ga_s, 3)
-    for i, src in enumerate((tq, tk, tv)):
-        temporal_out(src, i)
     attention_gradient(1, gt, wt, loads[6], ga_t)
     temporal_out(ga_t, 3)
 
@@ -213,6 +213,27 @@
 
     lax.fori_loop(0, heads, spatial_forward, 0)
     spatial_back(0, ah_s)
+
+    def temporal_load(i, h):
+        return tr[i, :, :, pl.ds(h * 128, 128)].reshape(256, 128)
+
+    def temporal_store(j, h, value):
+        to[j, :, :, pl.ds(h * 128, 128)] = value.astype(BF).reshape(16, 16, 128)
+
+    for i in range(3):
+        await_bytes(tr.at[i], t_in.at[i])
+    same_patch = lax.rem(lax.broadcasted_iota(jnp.int32, (256, 256), 0), 16) == lax.rem(
+        lax.broadcasted_iota(jnp.int32, (256, 256), 1), 16
+    )
+    for h in range(6):
+        scores = dot(temporal_load(0, h), temporal_load(1, h), NT) * SCALE
+        scores = jnp.where(same_patch, scores, -1e30)
+        expd = jnp.exp(scores - jnp.max(scores, axis=1, keepdims=True))
+        total = jnp.sum(expd, axis=1, keepdims=True)
+        low_prob = (expd * (1.0 / total)).astype(BF)
+        tprob[h] = low_prob
+        temporal_store(0, h, dot(low_prob, temporal_load(2, h), NN))
+    temporal_back(0, ah_t)
 
     spatial_arrived(3)
 
@@ -242,41 +263,23 @@
     for j, home in ((1, o_sq), (2, o_sk), (3, o_sv)):
         spatial_back(j, home)
 
-    for i in range(4):
-        await_bytes(tr.at[i], t_in.at[i])
-    same_patch = lax.rem(lax.broadcasted_iota(jnp.int32, (256, 256), 0), 16) == lax.rem(
-        lax.broadcasted_iota(jnp.int32, (256, 256), 1), 16
-    )
-
-    def temporal_head(h, carry):
-        c = pl.ds(aligned(h * 128, 128), 128)
-        queries, keys, values, grad = (tr[i, :, :, c].reshape(256, 128) for i in range(4))
-        scores = jnp.where(same_patch, dot(queries, keys, NT) * SCALE, -1e30)
-        expd = jnp.exp(scores - jnp.max(scores, axis=1, keepdims=True))
-        total = jnp.sum(expd, axis=1, keepdims=True)
-        probs = expd * (1.0 / total)
-        low_prob = probs.astype(BF)
-        attended = dot(low_prob, values, NN).astype(BF)
+    await_bytes(tr.at[3], t_in.at[3])
+    for h in range(6):
+        queries, keys, values, grad = (temporal_load(i, h) for i in range(4))
+        attended = to[0, :, :, pl.ds(h * 128, 128)].reshape(256, 128)
         row_dot = jnp.sum(grad.astype(F32) * attended.astype(F32), axis=1, keepdims=True)
-        grad_scores = (probs * (dot(grad, values, NT) - row_dot)).astype(BF)
-        out = (
-            attended,
-            (dot(grad_scores, keys, NN) * SCALE).astype(BF),
-            (dot(grad_scores, queries, TN) * SCALE).astype(BF),
-            dot(low_prob, grad, TN).astype(BF),
-        )
-        for j in range(4):
-            to[j, :, :, c] = out[j].reshape(16, 16, 128)
-        return carry
-
-    lax.fori_loop(0, 6, temporal_head, 0)
-    for j, home in ((0, ah_t), (1, o_tq), (2, o_tk), (3, o_tv)):
+        low_prob = tprob[h]
+        grad_scores = (low_prob.astype(F32) * (dot(grad, values, NT) - row_dot)).astype(BF)
+        temporal_store(1, h, dot(grad_scores, keys, NN) * SCALE)
+        temporal_store(2, h, dot(grad_scores, queries, TN) * SCALE)
+        temporal_store(3, h, dot(low_prob, grad, TN))
+    for j, home in ((1, o_tq), (2, o_tk), (3, o_tv)):
         temporal_back(j, home)
 
     def adapter(b, home, arrived, weight):
         await_bytes(home, arrived)
         rows = home[...].reshape(128, 1536)
-        small = dot(rows, down[...], NN).astype(BF)
+        small = dot(rows, down[...], NT).astype(BF)
         low[b] = small
 
         def step(n, carry):
@@ -354,15 +357,6 @@
 
     exchange(3, 8, ia, in_a, lambda j: b4, r4.at[pl.ds(aligned(ia * PART, 16), PART), :])
     await_bytes(r4, red_in.at[3])
-    for j in range(24):
-        c = pl.ds(j * 128, 128)
-        o_up[:, c] = r4[pl.ds(j * 80, 64), :].astype(F32)
-        tail = r4[pl.ds(j * 80 + 64, 16), :].astype(F32)
-        o_gs[:, c] = tail[0:1]
-        o_gt[:, c] = tail[1:2]
-    for j in range(12):
-        o_down[pl.ds(j * 128, 128), :] = r4[pl.ds(1920 + j * 64, 64), :].astype(F32).T
-
     for j, (s_ref, t_ref) in enumerate(((None, None), (o_sq, o_tq), (o_sk, o_tk), (o_sv, o_tv))):
         if j > 0:
             await_bytes(s_ref, s_home.at[j])
@@ -381,6 +375,33 @@
     await_bytes(acc.at[pl.ds(0, 15 * PIECE), :], red_out.at[1])
     await_bytes(acc.at[pl.ds(0, 15 * PIECE), :], red_out.at[2])
     await_bytes(pr.at[pl.ds(0, 7 * PART), :], red_out.at[3])
+
+
+def finish(*refs):
+    sources, r4, targets = refs[:6], refs[6], refs[7:13]
+    o_down, o_up, o_gs, o_gt, held, sem = refs[13:]
+    first = [
+        pltpu.make_async_copy(src, held.at[n], sem.at[0, n]) for n, src in enumerate(sources)
+    ]
+    second = [
+        pltpu.make_async_copy(held.at[n], dst, sem.at[1, n]) for n, dst in enumerate(targets)
+    ]
+    for copy in first:
+        copy.start()
+    for before, after in zip(first, second, strict=True):
+        before.wait()
+        after.start()
+    for j in range(24):
+        c = pl.ds(j * 128, 128)
+        o_up[:, c] = r4[pl.ds(j * 80, 64), :].astype(F32)
+        tail = r4[pl.ds(j * 80 + 64, 16), :].astype(F32)
+        o_gs[:, c] = tail[0:1]
+        o_gt[:, c] = tail[1:2]
+    for j in range(12):
+        o_down[:, pl.ds(j * 128, 128)] = r4[pl.ds(1920 + j * 64, 64), :].astype(F32)
+
+    for copy in second:
+        copy.wait()
 
 
 def shards(
@@ -403,15 +424,10 @@
     outs = pl.pallas_call(
         kernel,
         out_shape=(tokens,) * 6
-        + (
-            jax.ShapeDtypeStruct((1536, 64), F32),
-            jax.ShapeDtypeStruct((64, 3072), F32),
-            jax.ShapeDtypeStruct((1, 3072), F32),
-            jax.ShapeDtypeStruct((1, 3072), F32),
-        ),
+        + (jax.ShapeDtypeStruct((ROWS, 128), BF),),
         in_specs=[pl.BlockSpec(memory_space=pl.ANY)] * 13,
         out_specs=[pl.BlockSpec(memory_space=pl.ANY)] * 6
-        + [pl.BlockSpec(memory_space=pltpu.VMEM)] * 4,
+        + [pl.BlockSpec(memory_space=pltpu.VMEM)],
         scratch_shapes=[
             pltpu.VMEM((4, 1024, 256), BF),
             pltpu.VMEM((4, 1024, 256), BF),
@@ -419,10 +435,11 @@
             pltpu.VMEM((1024, 1024), BF),
             pltpu.VMEM((4, 16, 16, 768), BF),
             pltpu.VMEM((4, 16, 16, 768), BF),
+            pltpu.VMEM((6, 256, 256), BF),
             pltpu.VMEM((128, 3072), BF),
             pltpu.VMEM((1536, 3072), BF),
             pltpu.VMEM((1536, 3072), BF),
-            pltpu.VMEM((1536, 64), BF),
+            pltpu.VMEM((64, 1536), BF),
             pltpu.VMEM((64, 3072), BF),
             pltpu.VMEM((1, 3072), F32),
             pltpu.VMEM((1, 3072), F32),
@@ -441,7 +458,6 @@
             pltpu.VMEM((PIECE, 128), F32),
             pltpu.VMEM((16 * PIECE, 128), F32),
             pltpu.VMEM((PART, 128), BF),
-            pltpu.VMEM((ROWS, 128), BF),
             dma((7,)),
             dma((4,)),
             dma((4,)),
@@ -472,14 +488,30 @@
         output_gradient.reshape(128, 3072),
         spatial_projection,
         temporal_projection,
-        adapter_down,
+        adapter_down.T,
         adapter_up,
         spatial_channel_gate.reshape(1, 3072),
         temporal_channel_gate.reshape(1, 3072),
     )
+    outs = pl.pallas_call(
+        finish,
+        out_shape=(tokens,) * 6
+        + (
+            jax.ShapeDtypeStruct((64, 1536), F32),
+            jax.ShapeDtypeStruct((64, 3072), F32),
+            jax.ShapeDtypeStruct((1, 3072), F32),
+            jax.ShapeDtypeStruct((1, 3072), F32),
+        ),
+        in_specs=[pl.BlockSpec(memory_space=pltpu.HBM)] * 6
+        + [pl.BlockSpec(memory_space=pltpu.VMEM)],
+        out_specs=[pl.BlockSpec(memory_space=pltpu.HBM)] * 6
+        + [pl.BlockSpec(memory_space=pltpu.VMEM)] * 4,
+        scratch_shapes=[pltpu.VMEM((6, 2, 64, 1536), BF), dma((2, 6))],
+        compiler_params=pltpu.CompilerParams(vmem_limit_bytes=56 << 20),
+    )(*outs)
     return (
         *(array.reshape(1, 2, 64, 1536) for array in outs[:6]),
-        outs[6],
+        outs[6].T,
         outs[7],
         outs[8].reshape(3072),
         outs[9].reshape(3072),

time: 126 us -> 102 us (0.81)
  local copies, waits for them, and re-layouts: 19.3 us -> 0 us
  Pallas kernels: 103 us -> 99.8 us
    unnamed x11 -> x0, local copies, waits for them, and re-layouts: 19.3 us -> none
    pallas_call x1 -> x2, Pallas kernels: 103 us -> 99.8 us  [the longest x1 95.2 us: shards(): pl.pallas_call(kernel, out_shape=(tokens,) * 6 + (jax.ShapeDtypeStruct((R...]
where the time goes in v2:
time: 102 us; the launch traced here: 100 us
  Pallas kernels  99.8 us (98%)
    pallas_call x1, Pallas kernels, shards(): pl.pallas_call(kernel, out_shape=(tokens,) * 6 + (jax.ShapeDtypeStruct((R...  95.2 us
    pallas_call x1, Pallas kernels, shards(): pl.pallas_call(finish, out_shape=(tokens,) * 6 + (jax.ShapeDtypeStruct((6...  4.6 us

profile of v2, /device:TPU:0, one launch (start us, length us, event | category | flops | bytes accessed | tf_op | source)
XLA Modules:
  0.0 100.4 jit_solution(5979259181014513247)
XLA Ops:
  0.6 95.2 %shard_map.204 = (bf16[2,64,1536]{2,1,0:T(8,128)(2,1)}, bf16[2,64,1536]{2,1,0:T(8,128)(2,1)}, bf16[2,64,1536]{2,1,0:T(8,128)(2,1)}, bf16[2,64,1536]{2,1,0:T(8,12...) custom-call(bf16[2,64,1536]{2,1,0:T(8,128)(2,1)} %bitcast.20, ...), custom_call_target="tpu_custom_call" | custom-call | tf_op jit(solution)/shard_map/pallas_call | solution.py:424
  95.8 4.6 %shard_map.205 = (bf16[2,64,1536]{2,1,0:T(8,128)(2,1)}, bf16[2,64,1536]{2,1,0:T(8,128)(2,1)}, bf16[2,64,1536]{2,1,0:T(8,128)(2,1)}, bf16[2,64,1536]{2,1,0:T(8,12...) custom-call(bf16[2,64,1536]{2,1,0:T(8,128)(2,1)} %get-tuple-element., ...), custom_call_target="tpu_custom_call" | custom-call | tf_op jit(solution)/shard_map/pallas_call | solution.py:496

commit v3 on v2

--- a/solution.py
+++ b/solution.py
@@ -12,9 +12,9 @@
 NN = (((1,), (0,)), ((), ()))
 NT = (((1,), (1,)), ((), ()))
 TN = (((0,), (0,)), ((), ()))
-ROWS = 2688
-PART = 336
-PIECE = 24
+ROWS = 2560
+HALF = 1280
+PIECE = 80
 
 
 def dot(a, b, dims):
@@ -29,7 +29,7 @@
     sq, sk, sv, tq, tk, tv, og_hbm, ws_hbm, wt_hbm, down_hbm, up_hbm, gs_hbm, gt_hbm,
     o_sq, o_sk, o_sv, o_tq, o_tk, o_tv, r4,
     sr, so, prob, dsc, tr, to, tprob, og, ws, wt, down, up, gs, gt, gb, glow, ga_s, ga_t, ah_s, ah_t,
-    low, gate_rows, pr, r1, acc, r2, s2, r3, b4,
+    low, gate_rows, pr, r_core, half, r_yz, sum_yz, r_x, sum_x, r_all,
     load_sem, s_in, s_out, t_in, t_out, s_home, s_back, t_home, t_back, red_in, red_out,
 ):
     t = lax.axis_index("tm")
@@ -38,8 +38,9 @@
     core = lax.rem(s, 2)
     z = s // 4
     xh = lax.rem(chip, 2)
-    ia = z * 2 + core
-    ib = xh * 8 + t
+    xl = t // 4
+    y = lax.rem(t, 4)
+    plane = y * 4 + z
 
     loads = [
         pltpu.make_async_copy(src, dst, load_sem.at[n])
@@ -60,14 +61,20 @@
         return carry
 
     def greet_tm(n, carry):
-        other = lax.rem(t + n, 8)
-        greet((other, s))
-        greet((other, z * 4 + (1 - xh) * 2 + core))
+        greet((lax.rem(t + n, 8), s))
+        return carry
+
+    def greet_plane(n, carry):
+        other_y = lax.rem(y + 1 + n // 3, 4)
+        other_z = lax.rem(z + 1 + lax.rem(n, 3), 4)
+        greet((xl * 4 + other_y, other_z * 4 + xh * 2 + core))
         return carry
 
     lax.fori_loop(1, 16, greet_space, 0)
     lax.fori_loop(1, 8, greet_tm, 0)
-    pl.semaphore_wait(gate, 29)
+    lax.fori_loop(0, 9, greet_plane, 0)
+    greet(((1 - xl) * 4 + y, z * 4 + (1 - xh) * 2 + core))
+    pl.semaphore_wait(gate, 32)
 
     def start_local(src, dst, sem):
         pltpu.make_async_copy(src, dst, sem).start()
@@ -189,9 +196,7 @@
     for load in loads[:5]:
         load.wait()
     attention_gradient(0, gs, ws, loads[5], ga_s)
-    spatial_out(ga_s, 3)
     attention_gradient(1, gt, wt, loads[6], ga_t)
-    temporal_out(ga_t, 3)
 
     heads = 2 - core
     for i in range(3):
@@ -234,6 +239,70 @@
         tprob[h] = low_prob
         temporal_store(0, h, dot(low_prob, temporal_load(2, h), NN))
     temporal_back(0, ah_t)
+
+    spatial_out(ga_s, 3)
+    temporal_out(ga_t, 3)
+
+    def adapter(b, home, arrived, weight):
+        await_bytes(home, arrived)
+        rows = home[...].reshape(128, 1536)
+        small = dot(rows, down[...], NT).astype(BF)
+        low[b] = small
+
+        for n in range(6):
+            c = pl.ds(n * 512, 512)
+            branch = dot(rows, weight[:, c], NN) + dot(small, up[:, c], NN)
+            sums = jnp.sum(og[:, c].astype(F32) * branch, axis=0, keepdims=True)
+            for m in range(4):
+                gate_rows[pl.ds(b * 24 + n * 4 + m, 1), :] = sums[:, m * 128 : (m + 1) * 128]
+
+    adapter(0, ah_s, s_home.at[0], ws)
+    adapter(1, ah_t, t_home.at[0], wt)
+
+    low_st = low[0].astype(F32).T.astype(BF)
+    low_tt = low[1].astype(F32).T.astype(BF)
+    glow_st = glow[0].astype(F32).T.astype(BF)
+    glow_tt = glow[1].astype(F32).T.astype(BF)
+    for j in range(24):
+        c = pl.ds(j * 128, 128)
+        pr[pl.ds(j * 64, 64), :] = (
+            dot(low_st, gb[0, :, c], NN) + dot(low_tt, gb[1, :, c], NN)
+        ).astype(BF)
+    for j in range(12):
+        c = pl.ds(j * 128, 128)
+        pr[pl.ds(1536 + j * 64, 64), :] = (
+            dot(glow_st, ah_s[:, :, c].reshape(128, 128), NN)
+            + dot(glow_tt, ah_t[:, :, c].reshape(128, 128), NN)
+        ).astype(BF)
+    pr[pl.ds(2304, 48), :] = gate_rows[...].astype(BF)
+    pr[pl.ds(2352, ROWS - 2352), :] = jnp.zeros((ROWS - 2352, 128), BF)
+
+    other_core = (t, s + 1 - 2 * core)
+
+    def in_plane(j):
+        return (xl * 4 + j // 4, lax.rem(j, 4) * 4 + xh * 2 + core)
+
+    def to_plane(stage, src, dst):
+        def step(n, carry):
+            j = lax.rem(plane + n, 16)
+            start_remote(src(j), dst, red_out.at[stage], red_in.at[stage], in_plane(j))
+            return carry
+
+        lax.fori_loop(1, 16, step, 0)
+        start_local(src(plane), dst, red_in.at[stage])
+
+    start_remote(
+        pr.at[pl.ds(aligned((1 - core) * HALF, 16), HALF), :],
+        r_core,
+        red_out.at[0],
+        red_in.at[0],
+        other_core,
+    )
+
+    await_bytes(r_core, red_in.at[0])
+    mine = pr[pl.ds(aligned(core * HALF, 16), HALF), :].astype(F32)
+    half[...] = (mine + r_core[...].astype(F32)).astype(BF)
+    to_plane(1, lambda j: half.at[pl.ds(aligned(j * PIECE, 16), PIECE), :], r_yz.at[plane])
 
     spatial_arrived(3)
 
@@ -260,9 +329,8 @@
         return carry
 
     lax.fori_loop(0, heads, spatial_backward, 0)
-    for j, home in ((1, o_sq), (2, o_sk), (3, o_sv)):
-        spatial_back(j, home)
-
+
+    spatial_back(1, o_sq)
     await_bytes(tr.at[3], t_in.at[3])
     for h in range(6):
         queries, keys, values, grad = (temporal_load(i, h) for i in range(4))
@@ -273,90 +341,42 @@
         temporal_store(1, h, dot(grad_scores, keys, NN) * SCALE)
         temporal_store(2, h, dot(grad_scores, queries, TN) * SCALE)
         temporal_store(3, h, dot(low_prob, grad, TN))
-    for j, home in ((1, o_tq), (2, o_tk), (3, o_tv)):
-        temporal_back(j, home)
-
-    def adapter(b, home, arrived, weight):
-        await_bytes(home, arrived)
-        rows = home[...].reshape(128, 1536)
-        small = dot(rows, down[...], NT).astype(BF)
-        low[b] = small
-
-        def step(n, carry):
-            c = pl.ds(aligned(n * 512, 512), 512)
-            branch = dot(home[...].reshape(128, 1536), weight[:, c], NN) + dot(low[b], up[:, c], NN)
-            gate_rows[b, :, c] = jnp.sum(og[:, c].astype(F32) * branch, axis=0, keepdims=True)
-            return carry
-
-        lax.fori_loop(0, 6, step, 0)
-
-    adapter(0, ah_s, s_home.at[0], ws)
-    adapter(1, ah_t, t_home.at[0], wt)
-
-    low_st = low[0].astype(F32).T.astype(BF)
-    low_tt = low[1].astype(F32).T.astype(BF)
-    glow_st = glow[0].astype(F32).T.astype(BF)
-    glow_tt = glow[1].astype(F32).T.astype(BF)
-    line = lax.broadcasted_iota(jnp.int32, (16, 128), 0)
-    for j in range(24):
-        c = pl.ds(j * 128, 128)
-        pr[pl.ds(j * 80, 64), :] = (
-            dot(low_st, gb[0, :, c], NN) + dot(low_tt, gb[1, :, c], NN)
-        ).astype(BF)
-        pr[pl.ds(j * 80 + 64, 16), :] = jnp.where(
-            line == 0, gate_rows[0, :, c], jnp.where(line == 1, gate_rows[1, :, c], 0.0)
-        ).astype(BF)
-    for j in range(12):
-        c = pl.ds(j * 128, 128)
-        pr[pl.ds(1920 + j * 64, 64), :] = (
-            dot(glow_st, ah_s[:, :, c].reshape(128, 128), NN)
-            + dot(glow_tt, ah_t[:, :, c].reshape(128, 128), NN)
-        ).astype(BF)
-
-    def in_a(j):
-        return (t, (j // 2) * 4 + xh * 2 + lax.rem(j, 2))
-
-    def in_b(j):
-        return (lax.rem(j, 8), z * 4 + (j // 8) * 2 + core)
-
-    def exchange(stage, size, mine, device, src, dst):
-        def step(n, carry):
-            j = lax.rem(mine + n, size)
-            start_remote(src(j), dst, red_out.at[stage], red_in.at[stage], device(j))
-            return carry
-
-        lax.fori_loop(1, size, step, 0)
-        start_local(src(mine), dst, red_in.at[stage])
-
-    exchange(
-        0, 8, ia, in_a,
-        lambda j: pr.at[pl.ds(aligned(j * PART, 16), PART), :],
-        r1.at[ia],
-    )
-    await_bytes(r1, red_in.at[0])
-    total = r1[0].astype(F32)
-    for n in range(1, 8):
-        total = total + r1[n].astype(F32)
-    acc[pl.ds(0, PART), :] = total
-    acc[pl.ds(PART, 16 * PIECE - PART), :] = jnp.zeros((16 * PIECE - PART, 128), F32)
-
-    exchange(
-        1, 16, ib, in_b,
-        lambda j: acc.at[pl.ds(aligned(j * PIECE, 8), PIECE), :],
-        r2.at[ib],
-    )
-    await_bytes(r2, red_in.at[1])
-    total = r2[0]
+
+    temporal_back(1, o_tq)
+    await_bytes(r_yz, red_in.at[1])
+    total = r_yz[0].astype(F32)
     for n in range(1, 16):
-        total = total + r2[n]
-    s2[...] = total
-
-    exchange(2, 16, ib, in_b, lambda j: s2, r3.at[pl.ds(aligned(ib * PIECE, 8), PIECE), :])
-    await_bytes(r3, red_in.at[2])
-    b4[...] = r3[pl.ds(0, PART), :].astype(BF)
-
-    exchange(3, 8, ia, in_a, lambda j: b4, r4.at[pl.ds(aligned(ia * PART, 16), PART), :])
-    await_bytes(r4, red_in.at[3])
+        total = total + r_yz[n].astype(F32)
+    sum_yz[...] = total.astype(BF)
+    slot = r_x.at[xl * 2 + xh]
+    for flip_l, flip_h in ((0, 1), (1, 0), (1, 1)):
+        device_l = 1 - xl if flip_l else xl
+        device_h = 1 - xh if flip_h else xh
+        start_remote(
+            sum_yz,
+            slot,
+            red_out.at[2],
+            red_in.at[2],
+            (device_l * 4 + y, z * 4 + device_h * 2 + core),
+        )
+    start_local(sum_yz, slot, red_in.at[2])
+
+    spatial_back(2, o_sk)
+    spatial_back(3, o_sv)
+    temporal_back(2, o_tk)
+    temporal_back(3, o_tv)
+    await_bytes(r_x, red_in.at[2])
+    total = r_x[0].astype(F32)
+    for n in range(1, 4):
+        total = total + r_x[n].astype(F32)
+    sum_x[...] = total.astype(BF)
+    to_plane(3, lambda j: sum_x, r_all.at[pl.ds(aligned(plane * PIECE, 16), PIECE), :])
+    await_bytes(r_all, red_in.at[3])
+    rows = r4.at[pl.ds(aligned(core * HALF, 16), HALF), :]
+    start_remote(r_all, rows, red_out.at[4], red_in.at[4], other_core)
+    start_local(r_all, rows, red_in.at[4])
+    await_bytes(r4, red_in.at[4])
+
     for j, (s_ref, t_ref) in enumerate(((None, None), (o_sq, o_tq), (o_sk, o_tk), (o_sv, o_tv))):
         if j > 0:
             await_bytes(s_ref, s_home.at[j])
@@ -371,10 +391,8 @@
                 await_bytes(og.at[pl.ds(0, 64), pl.ds(0, 3072 - WIDTH[k])], s_out.at[i])
                 await_bytes(so.at[0, pl.ds(0, 960), pl.ds(0, WIDTH[k])], s_back.at[i])
 
-    await_bytes(pr.at[pl.ds(0, 7 * PART), :], red_out.at[0])
-    await_bytes(acc.at[pl.ds(0, 15 * PIECE), :], red_out.at[1])
-    await_bytes(acc.at[pl.ds(0, 15 * PIECE), :], red_out.at[2])
-    await_bytes(pr.at[pl.ds(0, 7 * PART), :], red_out.at[3])
+    for stage, rows in enumerate((HALF, 15 * PIECE, 3 * PIECE, 15 * PIECE, HALF)):
+        await_bytes(pr.at[pl.ds(0, rows), :], red_out.at[stage])
 
 
 def finish(*refs):
@@ -391,14 +409,14 @@
     for before, after in zip(first, second, strict=True):
         before.wait()
         after.start()
+    gates = r4[pl.ds(2304, 48), :].astype(F32)
     for j in range(24):
         c = pl.ds(j * 128, 128)
-        o_up[:, c] = r4[pl.ds(j * 80, 64), :].astype(F32)
-        tail = r4[pl.ds(j * 80 + 64, 16), :].astype(F32)
-        o_gs[:, c] = tail[0:1]
-        o_gt[:, c] = tail[1:2]
+        o_up[:, c] = r4[pl.ds(j * 64, 64), :].astype(F32)
+        o_gs[:, c] = gates[j : j + 1]
+        o_gt[:, c] = gates[24 + j : 25 + j]
     for j in range(12):
-        o_down[:, pl.ds(j * 128, 128)] = r4[pl.ds(1920 + j * 64, 64), :].astype(F32)
+        o_down[:, pl.ds(j * 128, 128)] = r4[pl.ds(1536 + j * 64, 64), :].astype(F32)
 
     for copy in second:
         copy.wait()
@@ -450,14 +468,15 @@
             pltpu.VMEM((2, 64, 1536), BF),
             pltpu.VMEM((2, 64, 1536), BF),
             pltpu.VMEM((2, 128, 64), BF),
-            pltpu.VMEM((2, 1, 3072), F32),
+            pltpu.VMEM((48, 128), F32),
             pltpu.VMEM((ROWS, 128), BF),
-            pltpu.VMEM((8, PART, 128), BF),
-            pltpu.VMEM((16 * PIECE, 128), F32),
-            pltpu.VMEM((16, PIECE, 128), F32),
-            pltpu.VMEM((PIECE, 128), F32),
-            pltpu.VMEM((16 * PIECE, 128), F32),
-            pltpu.VMEM((PART, 128), BF),
+            pltpu.VMEM((HALF, 128), BF),
+            pltpu.VMEM((HALF, 128), BF),
+            pltpu.VMEM((16, PIECE, 128), BF),
+            pltpu.VMEM((PIECE, 128), BF),
+            pltpu.VMEM((4, PIECE, 128), BF),
+            pltpu.VMEM((PIECE, 128), BF),
+            pltpu.VMEM((HALF, 128), BF),
             dma((7,)),
             dma((4,)),
             dma((4,)),
@@ -467,8 +486,8 @@
             dma((4,)),
             dma((4,)),
             dma((4,)),
-            dma((4,)),
-            dma((4,)),
+            dma((5,)),
+            dma((5,)),
         ],
         compiler_params=pltpu.CompilerParams(
             collective_id=0, has_side_effects=True, vmem_limit_bytes=56 << 20

time: 102 us -> 88.4 us (0.87)
  Pallas kernels: 99.8 us -> 87.1 us
    pallas_call x1, Pallas kernels: 95.2 us -> 82.5 us  [shards(): pl.pallas_call(kernel, out_shape=(tokens,) * 6 + (jax.ShapeDtypeStruct((R...]
where the time goes in v3:
time: 88.4 us; the launch traced here: 87.8 us
  Pallas kernels  87.1 us (99%)
    pallas_call x1, Pallas kernels, shards(): pl.pallas_call(kernel, out_shape=(tokens,) * 6 + (jax.ShapeDtypeStruct((R...  82.5 us
    pallas_call x1, Pallas kernels, shards(): pl.pallas_call(finish, out_shape=(tokens,) * 6 + (jax.ShapeDtypeStruct((6...  4.59 us

profile of v3, /device:TPU:0, one launch (start us, length us, event | category | flops | bytes accessed | tf_op | source)
XLA Modules:
  0.0 87.8 jit_solution(167622894199256061)
XLA Ops:
  0.6 82.5 %shard_map.204 = (bf16[2,64,1536]{2,1,0:T(8,128)(2,1)}, bf16[2,64,1536]{2,1,0:T(8,128)(2,1)}, bf16[2,64,1536]{2,1,0:T(8,128)(2,1)}, bf16[2,64,1536]{2,1,0:T(8,12...) custom-call(bf16[2,64,1536]{2,1,0:T(8,128)(2,1)} %bitcast.20, ...), custom_call_target="tpu_custom_call" | custom-call | tf_op jit(solution)/shard_map/pallas_call | solution.py:442
  83.2 4.6 %shard_map.205 = (bf16[2,64,1536]{2,1,0:T(8,128)(2,1)}, bf16[2,64,1536]{2,1,0:T(8,128)(2,1)}, bf16[2,64,1536]{2,1,0:T(8,128)(2,1)}, bf16[2,64,1536]{2,1,0:T(8,12...) custom-call(bf16[2,64,1536]{2,1,0:T(8,128)(2,1)} %get-tuple-element., ...), custom_call_target="tpu_custom_call" | custom-call | tf_op jit(solution)/shard_map/pallas_call | solution.py:515

commit v4 on v3

--- a/solution.py
+++ b/solution.py
@@ -397,18 +397,13 @@
 
 def finish(*refs):
     sources, r4, targets = refs[:6], refs[6], refs[7:13]
-    o_down, o_up, o_gs, o_gt, held, sem = refs[13:]
-    first = [
-        pltpu.make_async_copy(src, held.at[n], sem.at[0, n]) for n, src in enumerate(sources)
+    o_down, o_up, o_gs, o_gt, sem = refs[13:]
+    copies = [
+        pltpu.make_async_copy(src, dst, sem.at[n])
+        for n, (src, dst) in enumerate(zip(sources, targets, strict=True))
     ]
-    second = [
-        pltpu.make_async_copy(held.at[n], dst, sem.at[1, n]) for n, dst in enumerate(targets)
-    ]
-    for copy in first:
+    for copy in copies:
         copy.start()
-    for before, after in zip(first, second, strict=True):
-        before.wait()
-        after.start()
     gates = r4[pl.ds(2304, 48), :].astype(F32)
     for j in range(24):
         c = pl.ds(j * 128, 128)
@@ -418,7 +413,7 @@
     for j in range(12):
         o_down[:, pl.ds(j * 128, 128)] = r4[pl.ds(1536 + j * 64, 64), :].astype(F32)
 
-    for copy in second:
+    for copy in copies:
         copy.wait()
 
 
@@ -441,11 +436,9 @@
     dma = pltpu.SemaphoreType.DMA
     outs = pl.pallas_call(
         kernel,
-        out_shape=(tokens,) * 6
-        + (jax.ShapeDtypeStruct((ROWS, 128), BF),),
+        out_shape=(pltpu.VMEM((2, 64, 1536), BF),) * 6 + (pltpu.VMEM((ROWS, 128), BF),),
         in_specs=[pl.BlockSpec(memory_space=pl.ANY)] * 13,
-        out_specs=[pl.BlockSpec(memory_space=pl.ANY)] * 6
-        + [pl.BlockSpec(memory_space=pltpu.VMEM)],
+        out_specs=[pl.BlockSpec(memory_space=pl.ANY)] * 7,
         scratch_shapes=[
             pltpu.VMEM((4, 1024, 256), BF),
             pltpu.VMEM((4, 1024, 256), BF),
@@ -521,12 +514,11 @@
             jax.ShapeDtypeStruct((1, 3072), F32),
             jax.ShapeDtypeStruct((1, 3072), F32),
         ),
-        in_specs=[pl.BlockSpec(memory_space=pltpu.HBM)] * 6
-        + [pl.BlockSpec(memory_space=pltpu.VMEM)],
+        in_specs=[pl.BlockSpec(memory_space=pltpu.VMEM)] * 7,
         out_specs=[pl.BlockSpec(memory_space=pltpu.HBM)] * 6
         + [pl.BlockSpec(memory_space=pltpu.VMEM)] * 4,
-        scratch_shapes=[pltpu.VMEM((6, 2, 64, 1536), BF), dma((2, 6))],
-        compiler_params=pltpu.CompilerParams(vmem_limit_bytes=56 << 20),
+        scratch_shapes=[dma((6,))],
+        compiler_params=pltpu.CompilerParams(vmem_limit_bytes=16 << 20),
     )(*outs)
     return (
         *(array.reshape(1, 2, 64, 1536) for array in outs[:6]),

time: 88.4 us -> 85.2 us (0.964)
  Pallas kernels: 87.1 us -> 84 us
    pallas_call x1, Pallas kernels: 4.59 us -> 2.46 us  [shards(): pl.pallas_call(finish, out_shape=(tokens,) * 6 + (jax.ShapeDtypeStruct((6...]
    pallas_call x1, Pallas kernels: 82.5 us -> 81.5 us  [shards(): pl.pallas_call(kernel, out_shape=(pltpu.VMEM((2, 64, 1536), BF),) * 6 + (...]
where the time goes in v4:
time: 85.2 us; the launch traced here: 84.7 us
  Pallas kernels  84 us (99%)
    pallas_call x1, Pallas kernels, shards(): pl.pallas_call(kernel, out_shape=(pltpu.VMEM((2, 64, 1536), BF),) * 6 + (...  81.5 us
    pallas_call x1, Pallas kernels, shards(): pl.pallas_call(finish, out_shape=(tokens,) * 6 + (jax.ShapeDtypeStruct((6...  2.46 us

profile of v4, /device:TPU:0, one launch (start us, length us, event | category | flops | bytes accessed | tf_op | source)
XLA Modules:
  0.0 84.7 jit_solution(18325919851487962773)
XLA Ops:
  0.6 81.5 %shard_map.204 = (bf16[2,64,1536]{2,1,0:T(8,128)(2,1)S(1)}, bf16[2,64,1536]{2,1,0:T(8,128)(2,1)S(1)}, bf16[2,64,1536]{2,1,0:T(8,128)(2,1)S(1)}, bf16[2,64,1536]{...) custom-call(bf16[2,64,1536]{2,1,0:T(8,128)(2,1)} %bitcast.20, ...), custom_call_target="tpu_custom_call" | custom-call | tf_op jit(solution)/shard_map/pallas_call | solution.py:437
  82.2 2.5 %shard_map.205 = (bf16[2,64,1536]{2,1,0:T(8,128)(2,1)}, bf16[2,64,1536]{2,1,0:T(8,128)(2,1)}, bf16[2,64,1536]{2,1,0:T(8,128)(2,1)}, bf16[2,64,1536]{2,1,0:T(8,12...) custom-call(bf16[2,64,1536]{2,1,0:T(8,128)(2,1)S(1)} %get-tuple-elem, ...), custom_call_target="tpu_custom_call" | custom-call | tf_op jit(solution)/shard_map/pallas_call | solution.py:508

commit v5 on v4

--- a/solution.py
+++ b/solution.py
@@ -27,9 +27,9 @@
 
 def kernel(
     sq, sk, sv, tq, tk, tv, og_hbm, ws_hbm, wt_hbm, down_hbm, up_hbm, gs_hbm, gt_hbm,
-    o_sq, o_sk, o_sv, o_tq, o_tk, o_tv, r4,
+    o_sq, o_sk, o_sv, o_tq, o_tk, o_tv, o_down, o_up, o_gs, o_gt,
     sr, so, prob, dsc, tr, to, tprob, og, ws, wt, down, up, gs, gt, gb, glow, ga_s, ga_t, ah_s, ah_t,
-    low, gate_rows, pr, r_core, half, r_yz, sum_yz, r_x, sum_x, r_all,
+    low, gate_rows, pr, r_core, half, r_yz, sum_yz, r_x, sum_x, r_all, r4,
     load_sem, s_in, s_out, t_in, t_out, s_home, s_back, t_home, t_back, red_in, red_out,
 ):
     t = lax.axis_index("tm")
@@ -240,8 +240,9 @@
         temporal_store(0, h, dot(low_prob, temporal_load(2, h), NN))
     temporal_back(0, ah_t)
 
+    temporal_out(ga_t, 3)
+
     spatial_out(ga_s, 3)
-    temporal_out(ga_t, 3)
 
     def adapter(b, home, arrived, weight):
         await_bytes(home, arrived)
@@ -257,6 +258,7 @@
                 gate_rows[pl.ds(b * 24 + n * 4 + m, 1), :] = sums[:, m * 128 : (m + 1) * 128]
 
     adapter(0, ah_s, s_home.at[0], ws)
+
     adapter(1, ah_t, t_home.at[0], wt)
 
     low_st = low[0].astype(F32).T.astype(BF)
@@ -298,6 +300,19 @@
         red_in.at[0],
         other_core,
     )
+
+    await_bytes(tr.at[3], t_in.at[3])
+    for h in range(6):
+        queries, keys, values, grad = (temporal_load(i, h) for i in range(4))
+        attended = to[0, :, :, pl.ds(h * 128, 128)].reshape(256, 128)
+        row_dot = jnp.sum(grad.astype(F32) * attended.astype(F32), axis=1, keepdims=True)
+        low_prob = tprob[h]
+        grad_scores = (low_prob.astype(F32) * (dot(grad, values, NT) - row_dot)).astype(BF)
+        temporal_store(1, h, dot(grad_scores, keys, NN) * SCALE)
+        temporal_store(2, h, dot(grad_scores, queries, TN) * SCALE)
+        temporal_store(3, h, dot(low_prob, grad, TN))
+
+    temporal_back(1, o_tq)
 
     await_bytes(r_core, red_in.at[0])
     mine = pr[pl.ds(aligned(core * HALF, 16), HALF), :].astype(F32)
@@ -331,18 +346,7 @@
     lax.fori_loop(0, heads, spatial_backward, 0)
 
     spatial_back(1, o_sq)
-    await_bytes(tr.at[3], t_in.at[3])
-    for h in range(6):
-        queries, keys, values, grad = (temporal_load(i, h) for i in range(4))
-        attended = to[0, :, :, pl.ds(h * 128, 128)].reshape(256, 128)
-        row_dot = jnp.sum(grad.astype(F32) * attended.astype(F32), axis=1, keepdims=True)
-        low_prob = tprob[h]
-        grad_scores = (low_prob.astype(F32) * (dot(grad, values, NT) - row_dot)).astype(BF)
-        temporal_store(1, h, dot(grad_scores, keys, NN) * SCALE)
-        temporal_store(2, h, dot(grad_scores, queries, TN) * SCALE)
-        temporal_store(3, h, dot(low_prob, grad, TN))
-
-    temporal_back(1, o_tq)
+
     await_bytes(r_yz, red_in.at[1])
     total = r_yz[0].astype(F32)
     for n in range(1, 16):
@@ -361,21 +365,35 @@
         )
     start_local(sum_yz, slot, red_in.at[2])
 
+    temporal_back(2, o_tk)
+
     spatial_back(2, o_sk)
+
     spatial_back(3, o_sv)
-    temporal_back(2, o_tk)
+
     temporal_back(3, o_tv)
+
     await_bytes(r_x, red_in.at[2])
     total = r_x[0].astype(F32)
     for n in range(1, 4):
         total = total + r_x[n].astype(F32)
     sum_x[...] = total.astype(BF)
     to_plane(3, lambda j: sum_x, r_all.at[pl.ds(aligned(plane * PIECE, 16), PIECE), :])
+
     await_bytes(r_all, red_in.at[3])
     rows = r4.at[pl.ds(aligned(core * HALF, 16), HALF), :]
     start_remote(r_all, rows, red_out.at[4], red_in.at[4], other_core)
     start_local(r_all, rows, red_in.at[4])
     await_bytes(r4, red_in.at[4])
+
+    gates = r4[pl.ds(2304, 48), :].astype(F32)
+    for j in range(24):
+        c = pl.ds(j * 128, 128)
+        o_up[:, c] = r4[pl.ds(j * 64, 64), :].astype(F32)
+        o_gs[:, c] = gates[j : j + 1]
+        o_gt[:, c] = gates[24 + j : 25 + j]
+    for j in range(12):
+        o_down[:, pl.ds(j * 128, 128)] = r4[pl.ds(1536 + j * 64, 64), :].astype(F32)
 
     for j, (s_ref, t_ref) in enumerate(((None, None), (o_sq, o_tq), (o_sk, o_tk), (o_sv, o_tv))):
         if j > 0:
@@ -396,23 +414,13 @@
 
 
 def finish(*refs):
-    sources, r4, targets = refs[:6], refs[6], refs[7:13]
-    o_down, o_up, o_gs, o_gt, sem = refs[13:]
+    count = len(refs) // 2
+    sem = refs[-1]
     copies = [
-        pltpu.make_async_copy(src, dst, sem.at[n])
-        for n, (src, dst) in enumerate(zip(sources, targets, strict=True))
+        pltpu.make_async_copy(refs[n], refs[count + n], sem.at[n]) for n in range(count)
     ]
     for copy in copies:
         copy.start()
-    gates = r4[pl.ds(2304, 48), :].astype(F32)
-    for j in range(24):
-        c = pl.ds(j * 128, 128)
-        o_up[:, c] = r4[pl.ds(j * 64, 64), :].astype(F32)
-        o_gs[:, c] = gates[j : j + 1]
-        o_gt[:, c] = gates[24 + j : 25 + j]
-    for j in range(12):
-        o_down[:, pl.ds(j * 128, 128)] = r4[pl.ds(1536 + j * 64, 64), :].astype(F32)
-
     for copy in copies:
         copy.wait()
 
@@ -432,13 +440,19 @@
     spatial_channel_gate,
     temporal_channel_gate,
 ):
-    tokens = jax.ShapeDtypeStruct((2, 64, 1536), BF)
+    results = (((2, 64, 1536), BF),) * 6 + (
+        ((64, 1536), F32),
+        ((64, 3072), F32),
+        ((1, 3072), F32),
+        ((1, 3072), F32),
+    )
     dma = pltpu.SemaphoreType.DMA
     outs = pl.pallas_call(
         kernel,
-        out_shape=(pltpu.VMEM((2, 64, 1536), BF),) * 6 + (pltpu.VMEM((ROWS, 128), BF),),
+        out_shape=tuple(pltpu.VMEM(shape, dtype) for shape, dtype in results),
         in_specs=[pl.BlockSpec(memory_space=pl.ANY)] * 13,
-        out_specs=[pl.BlockSpec(memory_space=pl.ANY)] * 7,
+        out_specs=[pl.BlockSpec(memory_space=pl.ANY)] * 6
+        + [pl.BlockSpec(memory_space=pltpu.VMEM)] * 4,
         scratch_shapes=[
             pltpu.VMEM((4, 1024, 256), BF),
             pltpu.VMEM((4, 1024, 256), BF),
@@ -470,6 +484,7 @@
             pltpu.VMEM((4, PIECE, 128), BF),
             pltpu.VMEM((PIECE, 128), BF),
             pltpu.VMEM((HALF, 128), BF),
+            pltpu.VMEM((ROWS, 128), BF),
             dma((7,)),
             dma((4,)),
             dma((4,)),
@@ -507,17 +522,10 @@
     )
     outs = pl.pallas_call(
         finish,
-        out_shape=(tokens,) * 6
-        + (
-            jax.ShapeDtypeStruct((64, 1536), F32),
-            jax.ShapeDtypeStruct((64, 3072), F32),
-            jax.ShapeDtypeStruct((1, 3072), F32),
-            jax.ShapeDtypeStruct((1, 3072), F32),
-        ),
-        in_specs=[pl.BlockSpec(memory_space=pltpu.VMEM)] * 7,
-        out_specs=[pl.BlockSpec(memory_space=pltpu.HBM)] * 6
-        + [pl.BlockSpec(memory_space=pltpu.VMEM)] * 4,
-        scratch_shapes=[dma((6,))],
+        out_shape=tuple(jax.ShapeDtypeStruct(shape, dtype) for shape, dtype in results),
+        in_specs=[pl.BlockSpec(memory_space=pltpu.VMEM)] * 10,
+        out_specs=[pl.BlockSpec(memory_space=pltpu.HBM)] * 10,
+        scratch_shapes=[dma((10,))],
         compiler_params=pltpu.CompilerParams(vmem_limit_bytes=16 << 20),
     )(*outs)
     return (

time: 85.2 us -> 83.6 us (0.981)
  Pallas kernels: 84 us -> 82.7 us
    pallas_call x2, Pallas kernels: 84 us -> 82.7 us  [the longest x1 80.8 us: shards(): pl.pallas_call(kernel, out_shape=tuple((pltpu.VMEM(shape, dtype) for shap...]
where the time goes in v5:
time: 83.6 us; the launch traced here: 83.5 us
  Pallas kernels  82.7 us (99%)
    pallas_call x1, Pallas kernels, shards(): pl.pallas_call(kernel, out_shape=tuple((pltpu.VMEM(shape, dtype) for shap...  80.8 us
    pallas_call x1, Pallas kernels, shards(): pl.pallas_call(finish, out_shape=tuple((jax.ShapeDtypeStruct(shape, dtype...  1.88 us

profile of v5, /device:TPU:0, one launch (start us, length us, event | category | flops | bytes accessed | tf_op | source)
XLA Modules:
  0.0 83.5 jit_solution(2462474672916347268)
XLA Ops:
  0.6 80.8 %shard_map.204 = (bf16[2,64,1536]{2,1,0:T(8,128)(2,1)S(1)}, bf16[2,64,1536]{2,1,0:T(8,128)(2,1)S(1)}, bf16[2,64,1536]{2,1,0:T(8,128)(2,1)S(1)}, bf16[2,64,1536]{...) custom-call(bf16[2,64,1536]{2,1,0:T(8,128)(2,1)} %bitcast.20, ...), custom_call_target="tpu_custom_call" | custom-call | tf_op jit(solution)/shard_map/pallas_call | solution.py:450
  81.5 1.9 %shard_map.205 = (bf16[2,64,1536]{2,1,0:T(8,128)(2,1)}, bf16[2,64,1536]{2,1,0:T(8,128)(2,1)}, bf16[2,64,1536]{2,1,0:T(8,128)(2,1)}, bf16[2,64,1536]{2,1,0:T(8,12...) custom-call(bf16[2,64,1536]{2,1,0:T(8,128)(2,1)S(1)} %get-tuple-elem, ...), custom_call_target="tpu_custom_call" | custom-call | tf_op jit(solution)/shard_map/pallas_call | solution.py:523

commit v6 on v5

--- a/solution.py
+++ b/solution.py
@@ -333,19 +333,25 @@
             )
             grad_prob = dot(grad, values, NT)
             grad_scores = (prob[h, r, :].astype(F32) * (grad_prob - row_dot)).astype(BF)
-            dsc[r, :] = grad_scores
+            dsc[h, r, :] = grad_scores
             so[1, r, c] = (dot(grad_scores, keys, NN) * SCALE).astype(BF)
+        return carry
+
+    lax.fori_loop(0, heads, spatial_backward, 0)
+    spatial_back(1, o_sq)
+
+    def spatial_keys_values(h, carry):
+        c = pl.ds(aligned(h * 128, 128), 128)
         queries_t = sr[0, :, c].T
         grads_t = sr[3, :, c].T
         for n in range(4):
             r = pl.ds(n * 256, 256)
-            so[2, r, c] = (dot(queries_t, dsc[:, r], NN) * SCALE).T.astype(BF)
+            so[2, r, c] = (dot(queries_t, dsc[h, :, r], NN) * SCALE).T.astype(BF)
             so[3, r, c] = dot(grads_t, prob[h, :, r], NN).T.astype(BF)
         return carry
 
-    lax.fori_loop(0, heads, spatial_backward, 0)
-
-    spatial_back(1, o_sq)
+    lax.fori_loop(0, heads, spatial_keys_values, 0)
+
 
     await_bytes(r_yz, red_in.at[1])
     total = r_yz[0].astype(F32)
@@ -457,7 +463,7 @@
             pltpu.VMEM((4, 1024, 256), BF),
             pltpu.VMEM((4, 1024, 256), BF),
             pltpu.VMEM((2, 1024, 1024), BF),
-            pltpu.VMEM((1024, 1024), BF),
+            pltpu.VMEM((2, 1024, 1024), BF),
             pltpu.VMEM((4, 16, 16, 768), BF),
             pltpu.VMEM((4, 16, 16, 768), BF),
             pltpu.VMEM((6, 256, 256), BF),

time: 83.6 us -> 82.8 us (level)
  no operation moved by 1% of the time
where the time goes in v6:
time: 82.8 us; the launch traced here: 82.6 us
  Pallas kernels  82 us (99%)
    pallas_call x1, Pallas kernels, shards(): pl.pallas_call(kernel, out_shape=tuple((pltpu.VMEM(shape, dtype) for shap...  80.1 us
    pallas_call x1, Pallas kernels, shards(): pl.pallas_call(finish, out_shape=tuple((jax.ShapeDtypeStruct(shape, dtype...  1.88 us

profile of v6, /device:TPU:0, one launch (start us, length us, event | category | flops | bytes accessed | tf_op | source)
XLA Modules:
  0.0 82.6 jit_solution(5880900814585943304)
XLA Ops:
  0.6 80.1 %shard_map.204 = (bf16[2,64,1536]{2,1,0:T(8,128)(2,1)S(1)}, bf16[2,64,1536]{2,1,0:T(8,128)(2,1)S(1)}, bf16[2,64,1536]{2,1,0:T(8,128)(2,1)S(1)}, bf16[2,64,1536]{...) custom-call(bf16[2,64,1536]{2,1,0:T(8,128)(2,1)} %bitcast.20, ...), custom_call_target="tpu_custom_call" | custom-call | tf_op jit(solution)/shard_map/pallas_call | solution.py:456
  80.7 1.9 %shard_map.205 = (bf16[2,64,1536]{2,1,0:T(8,128)(2,1)}, bf16[2,64,1536]{2,1,0:T(8,128)(2,1)}, bf16[2,64,1536]{2,1,0:T(8,128)(2,1)}, bf16[2,64,1536]{2,1,0:T(8,12...) custom-call(bf16[2,64,1536]{2,1,0:T(8,128)(2,1)S(1)} %get-tuple-elem, ...), custom_call_target="tpu_custom_call" | custom-call | tf_op jit(solution)/shard_map/pallas_call | solution.py:529
